TPU v7x, 128 devices: a whole 4x4x4 slice. The times are simulated.
128 devices in a mesh: ctx: 16 (over x_lo, z, core), wsh: 8 (over y, x_hi).
Axes of the slice: x: 4 (x_hi: 2, x_lo: 2; x = x_hi * 2 + x_lo), y: 4, z: 4, core: 2. Of those that a mesh axis runs over, the one named last changes fastest.
Arguments:
- inputs: bfloat16 [8, 2048, 2048], P('wsh', 'ctx'), may hold values from -6 to 6
- output_cotangent: bfloat16 [8, 2048, 2048], P('wsh', 'ctx'), may hold values from -6 to 6
- block_index_per_position: int32 [8, 2048], P('wsh'), may hold values from 0 to 15, never falling along the last dimension, each value on 1 to 256 neighbouring positions
- adapter_index_per_run: int32 [8, 16], P('wsh', 'ctx'), may hold values from 0 to 7
- norm_gain: bfloat16 [2048], P('wsh'), may hold values from 0.5 to 1.5
- norm_bias: bfloat16 [2048], P('wsh'), may hold values from -4 to 4
- query_weight: bfloat16 [2048, 2048], P('wsh'), may hold values from -0.125 to 0.125
- key_weight: bfloat16 [2048, 2048], P('wsh'), may hold values from -0.125 to 0.125
- value_weight: bfloat16 [2048, 2048], P('wsh'), may hold values from -0.125 to 0.125
- dense_weight: bfloat16 [2048, 2048], P('wsh'), may hold values from -0.5 to 0.5
- query_bias: bfloat16 [2048], P('wsh'), may hold values from -4 to 4
- key_bias: bfloat16 [2048], P('wsh'), may hold values from -4 to 4
- value_bias: bfloat16 [2048], P('wsh'), may hold values from -4 to 4
- dense_bias: bfloat16 [2048], P('wsh'), may hold values from -4 to 4
- feedforward_in_weight: bfloat16 [2048, 8192], P('wsh'), may hold values from -0.125 to 0.125
- feedforward_in_bias: bfloat16 [8192], P('wsh'), may hold values from -4 to 4
- feedforward_out_weight: bfloat16 [8192, 2048], P('wsh'), may hold values from -0.0625 to 0.0625
- feedforward_out_bias: bfloat16 [2048], P('wsh'), may hold values from -4 to 4
- adapter_attention_down: bfloat16 [8, 3, 16, 2048], P('wsh'), may hold values from -0.125 to 0.125
- adapter_attention_up: bfloat16 [8, 3, 16, 2048], P('wsh'), may hold values from -1.5 to 1.5
- adapter_dense_down: bfloat16 [8, 16, 2048], P('wsh'), may hold values from -0.5 to 0.5
- adapter_dense_up: bfloat16 [8, 16, 2048], P('wsh'), may hold values from -1.5 to 1.5
- adapter_feedforward_in_down: bfloat16 [8, 16, 2048], P('wsh'), may hold values from -0.125 to 0.125
- adapter_feedforward_in_up: bfloat16 [8, 16, 8192], P('wsh'), may hold values from -1.5 to 1.5
- adapter_feedforward_out_down: bfloat16 [8, 16, 8192], P('wsh'), may hold values from -0.0625 to 0.0625
- adapter_feedforward_out_up: bfloat16 [8, 16, 2048], P('wsh'), may hold values from -1.5 to 1.5
Outputs:
- outputs: bfloat16 [8, 2048, 2048], P('wsh', 'ctx')
- grad_inputs: bfloat16 [8, 2048, 2048], P('wsh', 'ctx')
- grad_down_qkv: float32 [8, 3, 16, 2048], P('wsh')
- grad_up_qkv: float32 [8, 3, 16, 2048], P('wsh')
- dense_down_gradient: float32 [8, 16, 2048], P('wsh')
- dense_up_gradient: float32 [8, 16, 2048], P('wsh')
- feedforward_in_down_gradient: float32 [8, 16, 2048], P('wsh')
- feedforward_in_up_gradient: float32 [8, 16, 8192], P('wsh')
- feedforward_out_down_gradient: float32 [8, 16, 8192], P('wsh')
- feedforward_out_up_gradient: float32 [8, 16, 2048], P('wsh')
Inputs may be any that keep to these rules, and one draw needn't show every extreme that they name: `block_index_per_position`: block numbers never fall along a sequence; each block holds 1 to 256 positions and one holds exactly 256.
All inputs are finite; a program needn't handle non-finite values.
Results may differ from a plain program's by a relative error of at most 0.02.
Values may be sent and summed in bfloat16 or wider, within the bound.
No kernel may reach another device: no remote copies, remote signals or barrier semaphores. Data moves between devices by JAX's collectives and lax.ppermute only.
A program may use at most 320 MiB of HBM per device.

v0:
```python
import jax
import jax.numpy as jnp
from jax import lax
from jax.sharding import PartitionSpec as P

HEADS = 32
HEAD_DIM = 64
ROT = 32
ADAPTER_COUNT = 8


EPSILON = 1e-05
GELU_SCALE = 0.7978845608028654
NEGATIVE = -1e30


def gelu_tanh(values):
    return (
        0.5 * values * (1.0 + jnp.tanh(GELU_SCALE * (values + 0.044715 * values * values * values)))
    )


def layer_norm(values, gain, shift):
    center = values - jnp.mean(values, axis=-1, keepdims=True)
    spread = jnp.mean(center * center, axis=-1, keepdims=True)
    return center * lax.rsqrt(spread + EPSILON) * gain + shift


def rotate(field, positions, direction):
    token_count = field.shape[0]
    shaped = field.reshape(token_count, HEADS, HEAD_DIM)
    middle = ROT // 2
    rates = 10000.0 ** (-2.0 * jnp.arange(middle, dtype=jnp.float32) / ROT)
    angles = positions.astype(jnp.float32)[:, None] * rates[None, :]
    cosine = jnp.cos(angles)[:, None, :]
    sine = direction * jnp.sin(angles)[:, None, :]
    leading = shaped[:, :, :middle]
    trailing = shaped[:, :, middle:ROT]
    turned = jnp.concatenate(
        [
            leading * cosine - trailing * sine,
            trailing * cosine + leading * sine,
            shaped[:, :, ROT:],
        ],
        axis=2,
    )
    return turned.reshape(token_count, HEADS * HEAD_DIM)


def contract_last(left, right):
    return lax.dot_general(
        left, right, (((1,), (1,)), ((), ())), preferred_element_type=jnp.float32
    )


def contract_first(left, right):
    return lax.dot_general(
        left, right, (((0,), (0,)), ((), ())), preferred_element_type=jnp.float32
    )


def adapter_projection(lowrank_input_rows, weight_matrix, bias_vector, down_matrix, up_matrix):
    inner = contract_last(lowrank_input_rows, down_matrix).astype(jnp.bfloat16)
    result = jnp.dot(
        lowrank_input_rows, weight_matrix, preferred_element_type=jnp.float32
    ) + bias_vector.astype(jnp.float32)
    return (result + jnp.dot(inner, up_matrix, preferred_element_type=jnp.float32), inner)


def adapter_backward(
    lowrank_gradient,
    lowrank_input_rows,
    lowrank_inner_product,
    weight_matrix,
    down_matrix,
    up_matrix,
):
    inner_grad = contract_last(lowrank_gradient, up_matrix).astype(jnp.bfloat16)
    grad_in = contract_last(lowrank_gradient, weight_matrix) + jnp.dot(
        inner_grad, down_matrix, preferred_element_type=jnp.float32
    )
    grad_down = contract_first(inner_grad, lowrank_input_rows)
    grad_up = contract_first(lowrank_inner_product, lowrank_gradient)
    return (grad_in, grad_down, grad_up)


def add_rows(buffer, term, offset):
    current = lax.dynamic_slice_in_dim(buffer, offset, term.shape[0], 0)
    return lax.dynamic_update_slice_in_dim(buffer, current + term, offset, 0)


def local(
    inputs,
    output_cotangent,
    block_index_per_position,
    adapter_index_per_run,
    norm_gain,
    norm_bias,
    query_weight,
    key_weight,
    value_weight,
    dense_weight,
    query_bias,
    key_bias,
    value_bias,
    dense_bias,
    feedforward_in_weight,
    feedforward_in_bias,
    feedforward_out_weight,
    feedforward_out_bias,
    adapter_attention_down,
    adapter_attention_up,
    adapter_dense_down,
    adapter_dense_up,
    adapter_feedforward_in_down,
    adapter_feedforward_in_up,
    adapter_feedforward_out_down,
    adapter_feedforward_out_up,
):
    attention_weights_set = (
        lax.all_gather(norm_gain, "wsh", axis=0, tiled=True),
        lax.all_gather(norm_bias, "wsh", axis=0, tiled=True),
        lax.all_gather(query_weight, "wsh", axis=0, tiled=True),
        lax.all_gather(key_weight, "wsh", axis=0, tiled=True),
        lax.all_gather(value_weight, "wsh", axis=0, tiled=True),
        lax.all_gather(dense_weight, "wsh", axis=0, tiled=True),
        lax.all_gather(query_bias, "wsh", axis=0, tiled=True),
        lax.all_gather(key_bias, "wsh", axis=0, tiled=True),
        lax.all_gather(value_bias, "wsh", axis=0, tiled=True),
        lax.all_gather(dense_bias, "wsh", axis=0, tiled=True),
        lax.all_gather(adapter_attention_down, "wsh", axis=0, tiled=True),
        lax.all_gather(adapter_attention_up, "wsh", axis=0, tiled=True),
        lax.all_gather(adapter_dense_down, "wsh", axis=0, tiled=True),
        lax.all_gather(adapter_dense_up, "wsh", axis=0, tiled=True),
    )
    mlp_set = (
        lax.all_gather(feedforward_in_weight, "wsh", axis=0, tiled=True),
        lax.all_gather(feedforward_in_bias, "wsh", axis=0, tiled=True),
        lax.all_gather(feedforward_out_weight, "wsh", axis=0, tiled=True),
        lax.all_gather(feedforward_out_bias, "wsh", axis=0, tiled=True),
        lax.all_gather(adapter_feedforward_in_down, "wsh", axis=0, tiled=True),
        lax.all_gather(adapter_feedforward_in_up, "wsh", axis=0, tiled=True),
        lax.all_gather(adapter_feedforward_out_down, "wsh", axis=0, tiled=True),
        lax.all_gather(adapter_feedforward_out_up, "wsh", axis=0, tiled=True),
    )
    chosen = adapter_index_per_run[0, 0]

    def pick(stack):
        return lax.dynamic_index_in_dim(stack, chosen, 0, keepdims=False)

    run_tokens = inputs.shape[1]
    length = block_index_per_position.shape[1]
    place = lax.axis_index("ctx")
    positions = place * run_tokens + jnp.arange(run_tokens, dtype=jnp.int32)
    block_row = block_index_per_position[0]
    query_ids = lax.dynamic_slice_in_dim(block_row, place * run_tokens, run_tokens)
    last_own = query_ids[run_tokens - 1]
    score_scale = HEAD_DIM ** (-0.5)
    source = inputs[0].astype(jnp.float32)
    gain_f = attention_weights_set[0].astype(jnp.float32)
    shift_f = attention_weights_set[1].astype(jnp.float32)
    normalized_lowrank = layer_norm(source, gain_f, shift_f).astype(jnp.bfloat16)
    attention_down_matrix = pick(attention_weights_set[10])
    attention_up_matrix = pick(attention_weights_set[11])
    query_preactivation, query_inner_product = adapter_projection(
        normalized_lowrank,
        attention_weights_set[2],
        attention_weights_set[6],
        attention_down_matrix[0],
        attention_up_matrix[0],
    )
    key_preactivation, key_inner_product = adapter_projection(
        normalized_lowrank,
        attention_weights_set[3],
        attention_weights_set[7],
        attention_down_matrix[1],
        attention_up_matrix[1],
    )
    value_preactivation, value_inner_product = adapter_projection(
        normalized_lowrank,
        attention_weights_set[4],
        attention_weights_set[8],
        attention_down_matrix[2],
        attention_up_matrix[2],
    )
    query_low = rotate(query_preactivation, positions, 1.0).astype(jnp.bfloat16)
    key_low = rotate(key_preactivation, positions, 1.0).astype(jnp.bfloat16)
    value_low = value_preactivation.astype(jnp.bfloat16)
    query_heads = query_low.reshape(run_tokens, HEADS, HEAD_DIM)

    def attend_block(running, keys_blk, values_blk, offset):
        largest, totals, summed = running
        scores = (
            jnp.einsum("thd,shd->hts", query_heads, keys_blk, preferred_element_type=jnp.float32)
            * score_scale
        )
        key_ids = lax.dynamic_slice_in_dim(block_row, offset, keys_blk.shape[0])
        allowed = (key_ids[None, :] <= query_ids[:, None])[None]
        scores = jnp.where(allowed, scores, NEGATIVE)
        new_largest = jnp.maximum(largest, jnp.max(scores, axis=2))
        weights = jnp.where(allowed, jnp.exp(scores - new_largest[:, :, None]), 0.0)
        factor = jnp.exp(largest - new_largest)
        totals = totals * factor + jnp.sum(weights, axis=2)
        summed = summed * factor[:, :, None] + jnp.einsum(
            "hts,shd->htd",
            weights.astype(jnp.bfloat16),
            values_blk,
            preferred_element_type=jnp.float32,
        )
        return (new_largest, totals, summed)

    initial = (
        jnp.full((HEADS, run_tokens), NEGATIVE, jnp.float32),
        jnp.zeros((HEADS, run_tokens), jnp.float32),
        jnp.zeros((HEADS, run_tokens, HEAD_DIM), jnp.float32),
    )
    running = initial
    key_piece = lax.all_gather(key_low, "ctx", axis=0, tiled=True)
    value_piece = lax.all_gather(value_low, "ctx", axis=0, tiled=True)
    piece_rows = key_piece.shape[0]
    block_rows = 512
    block_count = piece_rows // block_rows
    keys_blocks = key_piece.reshape(block_count, block_rows, HEADS, HEAD_DIM)
    values_blocks = value_piece.reshape(block_count, block_rows, HEADS, HEAD_DIM)
    offsets = block_rows * jnp.arange(block_count, dtype=jnp.int32)

    def fold_visit(carried, element):
        keys_blk, values_blk, start = element
        first_key = lax.dynamic_index_in_dim(block_row, start, 0, keepdims=False)

        def fold_work(state):
            return attend_block(state, keys_blk, values_blk, start)

        return (lax.cond(first_key > last_own, lambda state: state, fold_work, carried), None)

    running, unused = lax.scan(fold_visit, running, (keys_blocks, values_blocks, offsets))
    largest, totals, summed = running
    attn_heads = summed / totals[:, :, None]
    logsum = largest + jnp.log(totals)
    attn_low = (
        attn_heads.transpose(1, 0, 2).reshape(run_tokens, HEADS * HEAD_DIM).astype(jnp.bfloat16)
    )
    attention_output, dense_inner_product = adapter_projection(
        attn_low,
        attention_weights_set[5],
        attention_weights_set[9],
        pick(attention_weights_set[12]),
        pick(attention_weights_set[13]),
    )
    feedforward_preactivation, feedforward_in_inner = adapter_projection(
        normalized_lowrank, mlp_set[0], mlp_set[1], pick(mlp_set[4]), pick(mlp_set[5])
    )
    act_low = gelu_tanh(feedforward_preactivation).astype(jnp.bfloat16)
    feedforward_output, feedforward_out_inner = adapter_projection(
        act_low, mlp_set[2], mlp_set[3], pick(mlp_set[6]), pick(mlp_set[7])
    )
    outputs = (source + attention_output + feedforward_output).astype(jnp.bfloat16)[None]
    attention_weights_set = (
        lax.all_gather(norm_gain, "wsh", axis=0, tiled=True),
        lax.all_gather(norm_bias, "wsh", axis=0, tiled=True),
        lax.all_gather(query_weight, "wsh", axis=0, tiled=True),
        lax.all_gather(key_weight, "wsh", axis=0, tiled=True),
        lax.all_gather(value_weight, "wsh", axis=0, tiled=True),
        lax.all_gather(dense_weight, "wsh", axis=0, tiled=True),
        lax.all_gather(query_bias, "wsh", axis=0, tiled=True),
        lax.all_gather(key_bias, "wsh", axis=0, tiled=True),
        lax.all_gather(value_bias, "wsh", axis=0, tiled=True),
        lax.all_gather(dense_bias, "wsh", axis=0, tiled=True),
        lax.all_gather(adapter_attention_down, "wsh", axis=0, tiled=True),
        lax.all_gather(adapter_attention_up, "wsh", axis=0, tiled=True),
        lax.all_gather(adapter_dense_down, "wsh", axis=0, tiled=True),
        lax.all_gather(adapter_dense_up, "wsh", axis=0, tiled=True),
    )
    mlp_set = (
        lax.all_gather(feedforward_in_weight, "wsh", axis=0, tiled=True),
        lax.all_gather(feedforward_in_bias, "wsh", axis=0, tiled=True),
        lax.all_gather(feedforward_out_weight, "wsh", axis=0, tiled=True),
        lax.all_gather(feedforward_out_bias, "wsh", axis=0, tiled=True),
        lax.all_gather(adapter_feedforward_in_down, "wsh", axis=0, tiled=True),
        lax.all_gather(adapter_feedforward_in_up, "wsh", axis=0, tiled=True),
        lax.all_gather(adapter_feedforward_out_down, "wsh", axis=0, tiled=True),
        lax.all_gather(adapter_feedforward_out_up, "wsh", axis=0, tiled=True),
    )
    lowrank_gradient = output_cotangent[0]
    grad_source = lowrank_gradient.astype(jnp.float32)
    activation_gradient, feedforward_out_down_gradient, feedforward_out_up_gradient = (
        adapter_backward(
            lowrank_gradient,
            act_low,
            feedforward_out_inner,
            mlp_set[2],
            pick(mlp_set[6]),
            pick(mlp_set[7]),
        )
    )
    unused, gelu_pull = jax.vjp(gelu_tanh, feedforward_preactivation)
    grad_fc1_low = gelu_pull(activation_gradient)[0].astype(jnp.bfloat16)
    normalized_gradient, feedforward_in_down_gradient, feedforward_in_up_gradient = (
        adapter_backward(
            grad_fc1_low,
            normalized_lowrank,
            feedforward_in_inner,
            mlp_set[0],
            pick(mlp_set[4]),
            pick(mlp_set[5]),
        )
    )
    attention_gradient, dense_down_gradient, dense_up_gradient = adapter_backward(
        lowrank_gradient,
        attn_low,
        dense_inner_product,
        attention_weights_set[5],
        pick(attention_weights_set[12]),
        pick(attention_weights_set[13]),
    )
    grad_flat = attention_gradient.astype(jnp.bfloat16)
    grad_heads = grad_flat.reshape(run_tokens, HEADS, HEAD_DIM)
    deltas = jnp.einsum("thd,htd->ht", grad_heads.astype(jnp.float32), attn_heads)
    zero_query = jnp.zeros((run_tokens, HEADS, HEAD_DIM), jnp.float32)
    back_initial = (
        zero_query,
        jnp.zeros((length, HEADS, HEAD_DIM), jnp.float32),
        jnp.zeros((length, HEADS, HEAD_DIM), jnp.float32),
    )
    running_back = back_initial
    key_piece = lax.all_gather(key_low, "ctx", axis=0, tiled=True)
    value_piece = lax.all_gather(value_low, "ctx", axis=0, tiled=True)
    piece_rows = key_piece.shape[0]
    block_rows = 512
    block_count = piece_rows // block_rows
    keys_blocks = key_piece.reshape(block_count, block_rows, HEADS, HEAD_DIM)
    values_blocks = value_piece.reshape(block_count, block_rows, HEADS, HEAD_DIM)
    offsets = block_rows * jnp.arange(block_count, dtype=jnp.int32)

    def key_visit(carried, element):
        keys_blk, values_blk, start = element
        first_key = lax.dynamic_index_in_dim(block_row, start, 0, keepdims=False)

        def key_work(state):
            scores = (
                jnp.einsum(
                    "thd,shd->hts", query_heads, keys_blk, preferred_element_type=jnp.float32
                )
                * score_scale
            )
            key_ids = lax.dynamic_slice_in_dim(block_row, start, block_rows)
            allowed = (key_ids[None, :] <= query_ids[:, None])[None]
            scores = jnp.where(allowed, scores, NEGATIVE)
            probs = jnp.where(allowed, jnp.exp(scores - logsum[:, :, None]), 0.0)
            grad_probs = jnp.einsum(
                "thd,shd->hts", grad_heads, values_blk, preferred_element_type=jnp.float32
            )
            grad_scores = (probs * (grad_probs - deltas[:, :, None])).astype(jnp.bfloat16)
            grad_query = (
                state[0]
                + jnp.einsum(
                    "hts,shd->thd", grad_scores, keys_blk, preferred_element_type=jnp.float32
                )
                * score_scale
            )
            grad_values = jnp.einsum(
                "hts,thd->shd",
                probs.astype(jnp.bfloat16),
                grad_heads,
                preferred_element_type=jnp.float32,
            )
            grad_keys = (
                jnp.einsum(
                    "hts,thd->shd", grad_scores, query_heads, preferred_element_type=jnp.float32
                )
                * score_scale
            )
            return (
                grad_query,
                add_rows(state[1], grad_keys, start),
                add_rows(state[2], grad_values, start),
            )

        return (lax.cond(first_key > last_own, lambda state: state, key_work, carried), None)

    running_back, unused_out = lax.scan(
        key_visit, running_back, (keys_blocks, values_blocks, offsets)
    )
    grad_query = running_back[0]
    grad_key, grad_value = (
        lax.psum_scatter(
            running_back[1].reshape(length, HEADS * HEAD_DIM).astype(jnp.bfloat16),
            "ctx",
            scatter_dimension=0,
            tiled=True,
        ).astype(jnp.float32),
        lax.psum_scatter(
            running_back[2].reshape(length, HEADS * HEAD_DIM).astype(jnp.bfloat16),
            "ctx",
            scatter_dimension=0,
            tiled=True,
        ).astype(jnp.float32),
    )
    grad_query_low = rotate(
        grad_query.reshape(run_tokens, HEADS * HEAD_DIM), positions, -1.0
    ).astype(jnp.bfloat16)
    grad_key_low = rotate(grad_key, positions, -1.0).astype(jnp.bfloat16)
    grad_value_low = grad_value.astype(jnp.bfloat16)
    attention_down_matrix = pick(attention_weights_set[10])
    attention_up_matrix = pick(attention_weights_set[11])
    gradient_via_query, query_down_matrix, query_up_matrix = adapter_backward(
        grad_query_low,
        normalized_lowrank,
        query_inner_product,
        attention_weights_set[2],
        attention_down_matrix[0],
        attention_up_matrix[0],
    )
    gradient_via_key, key_down_matrix, key_up_matrix = adapter_backward(
        grad_key_low,
        normalized_lowrank,
        key_inner_product,
        attention_weights_set[3],
        attention_down_matrix[1],
        attention_up_matrix[1],
    )
    gradient_via_value, value_down_matrix, value_up_matrix = adapter_backward(
        grad_value_low,
        normalized_lowrank,
        value_inner_product,
        attention_weights_set[4],
        attention_down_matrix[2],
        attention_up_matrix[2],
    )
    grad_hidden = gradient_via_query + gradient_via_key + gradient_via_value + normalized_gradient
    gain_back = attention_weights_set[0].astype(jnp.float32)
    shift_back = attention_weights_set[1].astype(jnp.float32)

    def norm_only(values):
        return layer_norm(values, gain_back, shift_back)

    unused, norm_pull = jax.vjp(norm_only, source)
    grad_inputs = (grad_source + norm_pull(grad_hidden)[0]).astype(jnp.bfloat16)[None]
    selector = (jnp.arange(ADAPTER_COUNT, dtype=jnp.int32) == chosen).astype(jnp.float32)

    def spread_out(gradient):
        return selector.reshape((ADAPTER_COUNT,) + (1,) * gradient.ndim) * gradient[None]

    shares = (
        lax.psum_scatter(
            spread_out(jnp.stack([query_down_matrix, key_down_matrix, value_down_matrix])).astype(
                jnp.bfloat16
            ),
            "wsh",
            scatter_dimension=0,
            tiled=True,
        ).astype(jnp.float32),
        lax.psum_scatter(
            spread_out(jnp.stack([query_up_matrix, key_up_matrix, value_up_matrix])).astype(
                jnp.bfloat16
            ),
            "wsh",
            scatter_dimension=0,
            tiled=True,
        ).astype(jnp.float32),
        lax.psum_scatter(
            spread_out(dense_down_gradient).astype(jnp.bfloat16),
            "wsh",
            scatter_dimension=0,
            tiled=True,
        ).astype(jnp.float32),
        lax.psum_scatter(
            spread_out(dense_up_gradient).astype(jnp.bfloat16),
            "wsh",
            scatter_dimension=0,
            tiled=True,
        ).astype(jnp.float32),
        lax.psum_scatter(
            spread_out(feedforward_in_down_gradient).astype(jnp.bfloat16),
            "wsh",
            scatter_dimension=0,
            tiled=True,
        ).astype(jnp.float32),
        lax.psum_scatter(
            spread_out(feedforward_in_up_gradient).astype(jnp.bfloat16),
            "wsh",
            scatter_dimension=0,
            tiled=True,
        ).astype(jnp.float32),
        lax.psum_scatter(
            spread_out(feedforward_out_down_gradient).astype(jnp.bfloat16),
            "wsh",
            scatter_dimension=0,
            tiled=True,
        ).astype(jnp.float32),
        lax.psum_scatter(
            spread_out(feedforward_out_up_gradient).astype(jnp.bfloat16),
            "wsh",
            scatter_dimension=0,
            tiled=True,
        ).astype(jnp.float32),
    )
    totals_out = (
        lax.psum(shares[0].astype(jnp.bfloat16), "ctx").astype(jnp.float32),
        lax.psum(shares[1].astype(jnp.bfloat16), "ctx").astype(jnp.float32),
        lax.psum(shares[2].astype(jnp.bfloat16), "ctx").astype(jnp.float32),
        lax.psum(shares[3].astype(jnp.bfloat16), "ctx").astype(jnp.float32),
        lax.psum(shares[4].astype(jnp.bfloat16), "ctx").astype(jnp.float32),
        lax.psum(shares[5].astype(jnp.bfloat16), "ctx").astype(jnp.float32),
        lax.psum(shares[6].astype(jnp.bfloat16), "ctx").astype(jnp.float32),
        lax.psum(shares[7].astype(jnp.bfloat16), "ctx").astype(jnp.float32),
    )
    return (
        outputs,
        grad_inputs,
        totals_out[0],
        totals_out[1],
        totals_out[2],
        totals_out[3],
        totals_out[4],
        totals_out[5],
        totals_out[6],
        totals_out[7],
    )


def solution(mesh):
    placed = (
        P("wsh", "ctx", None),
        P("wsh", "ctx", None),
        P("wsh", None),
        P("wsh", "ctx"),
        P("wsh"),
        P("wsh"),
        P("wsh", None),
        P("wsh", None),
        P("wsh", None),
        P("wsh", None),
        P("wsh"),
        P("wsh"),
        P("wsh"),
        P("wsh"),
        P("wsh", None),
        P("wsh"),
        P("wsh", None),
        P("wsh"),
        P("wsh", None, None, None),
        P("wsh", None, None, None),
        P("wsh", None, None),
        P("wsh", None, None),
        P("wsh", None, None),
        P("wsh", None, None),
        P("wsh", None, None),
        P("wsh", None, None),
    )
    return jax.shard_map(
        local,
        mesh=mesh,
        in_specs=placed,
        out_specs=(
            P("wsh", "ctx", None),
            P("wsh", "ctx", None),
            P("wsh", None, None, None),
            P("wsh", None, None, None),
            P("wsh", None, None),
            P("wsh", None, None),
            P("wsh", None, None),
            P("wsh", None, None),
            P("wsh", None, None),
            P("wsh", None, None),
        ),
        check_vma=False,
    )
```

profile of v0, /device:TPU:1, one launch (start us, length us, event | category | flops | bytes accessed | tf_op | source)
XLA Modules:
  0.0 2818.4 jit_solution(14310728355234572828)
XLA Ops:
  11.9 20.7 all-gather
  84.5 86.4 %all-gather.20.cloned.1.call-done = bf16[2048,2048]{1,0:T(8,128)(2,1)} async-done(((bf16[256,2048]{1,0:T(8,128)(2,1)}), bf16[2048,2048]{1,0:T(8,128)(2,1)}) %all-gather.20.cloned.1.call-update) | async-done | bytes 8388624 | tf_op jit(solution)/shard_map/all_gather | solution.py:124
  175.6 45.0 %all-gather.24.cloned.1.call-done = bf16[8,3,16,2048]{3,2,1,0:T(8,128)(2,1)} async-done(((bf16[1,3,16,2048]{3,2,1,0:T(8,128)(2,1)}), bf16[8,3,16,2048]{3,2,1,0:T(8,128)(2,1)}) %all-gather.24.cloned.1.call-update) | async-done | bytes 1572880 | tf_op jit(solution)/shard_map/all_gather | solution.py:132
  225.2 103.4 %all-gather.28.cloned.1.call-done = bf16[2048,2048]{1,0:T(8,128)(2,1)} async-done(((bf16[256,2048]{1,0:T(8,128)(2,1)}), bf16[2048,2048]{1,0:T(8,128)(2,1)}) %all-gather.28.cloned.1.call-update) | async-done | bytes 8388624 | tf_op jit(solution)/shard_map/all_gather | solution.py:123
  355.5 80.3 %all-gather.30.cloned.1.call-done = bf16[2048,2048]{1,0:T(8,128)(2,1)} async-done(((bf16[256,2048]{1,0:T(8,128)(2,1)}), bf16[2048,2048]{1,0:T(8,128)(2,1)}) %all-gather.30.cloned.1.call-update) | async-done | bytes 8388624 | tf_op jit(solution)/shard_map/all_gather | solution.py:125
  443.3 31.5 %all_gather.104 = bf16[8,16,2048]{2,1,0:T(8,128)(2,1)S(1)} all-gather(bf16[1,16,2048]{2,1,0:T(8,128)(2,1)S(1)} %copy-done.27), channel_id=1, replica_groups=mesh['ctx'=16,'wsh'=8] {'wsh'}, dimensions={0}, use_global_device_ids=true | all-gather | bytes 589824 | tf_op jit(solution)/shard_map/all_gather | solution.py:134
  474.8 32.0 %all_gather.103 = bf16[8,16,2048]{2,1,0:T(8,128)(2,1)S(1)} all-gather(bf16[1,16,2048]{2,1,0:T(8,128)(2,1)S(1)} %copy-done.28), channel_id=1, replica_groups=mesh['ctx'=16,'wsh'=8] {'wsh'}, dimensions={0}, use_global_device_ids=true | all-gather | bytes 589824 | tf_op jit(solution)/shard_map/all_gather | solution.py:133
  508.2 48.2 %all-gather.34.cloned.1.call-done = bf16[2048,2048]{1,0:T(8,128)(2,1)} async-done(((bf16[256,2048]{1,0:T(8,128)(2,1)}), bf16[2048,2048]{1,0:T(8,128)(2,1)}) %all-gather.34.cloned.1.call-update) | async-done | bytes 8388624 | tf_op jit(solution)/shard_map/all_gather | solution.py:126
  563.4 54.6 %all-gather.26.cloned.1.call-done = bf16[2048,2048]{0,1:T(8,128)(2,1)} async-done(((bf16[128,2048]{0,1:T(8,128)(2,1)}), bf16[2048,2048]{0,1:T(8,128)(2,1)}) %all-gather.26.cloned.1.call-update) | async-done | bytes 8388624 | tf_op jit(solution)/shard_map/all_gather | solution.py:218
  641.5 30.3 %all-gather.32.cloned.1.call-done = bf16[2048,2048]{1,0:T(8,128)(2,1)} async-done(((bf16[128,2048]{1,0:T(8,128)(2,1)}), bf16[2048,2048]{1,0:T(8,128)(2,1)}) %all-gather.32.cloned.1.call-update) | async-done | bytes 8388624 | tf_op jit(solution)/shard_map/all_gather | solution.py:219
  671.9 24.4 reshape.423
  714.7 30.4 %while.28 = (s32[]{:T(128)}, f32[32,128]{1,0:T(8,128)S(1)}, f32[32,128]{1,0:T(8,128)S(1)}, f32[32,128,64]{1,2,0:T(8,128)S(1)}, s32[4]{0:T(128)S(1)}, /*index=5*/...) while((s32[]{:T(128)}, f32[32,128]{1,0:T(8,128)S(1)}, ...), condition=%wide.region_7.8_spmd, body=%wide.region_2.7_spmd.sunk | while | flops 564731904 | bytes 32513908 | solution.py:236
  762.1 92.3 %while.29 = (s32[]{:T(128)}, f32[128,32,64]{0,2,1:T(8,128)S(1)}, f32[2048,32,64]{0,2,1:T(8,128)}, f32[2048,32,64]{0,2,1:T(8,128)}, s32[4]{0:T(128)S(1)}, /*index...) while((s32[]{:T(128)}, f32[128,32,64]{0,2,1:T(8,128)S(1)}, ...), condition=%wide.region_11.12_spmd, body=%wide.region_8.11_spmd.sunk | while | flops 1371078656 | bytes 132375024 | solution.py:381
  766.9 74.4 %conditional.5 = ((f32[128,32,64]{0,2,1:T(8,128)S(1)}, f32[2048,32,64]{0,2,1:T(8,128)}, f32[2048,32,64]{0,2,1:T(8,128)})) conditional(s32[]{:T(128)} %convert_element_type.434, (s32[]{:T(128)}, s32[2048]{0:T(1024)S(1)}, s32[128]{0:T(128)S(1)}, bf16[4,512,32,64]{1,3,2,0:T(8,128)(2,1)}, s32[]{:T(128)}, /*index=5*/bf16[128,32,64]{0,2,1:T(8,128)(2,1)S(1)}, ...), branch_computations={%region_9.9_spmd, %region_10.10_spmd} | conditional | flops 1371078656 | bytes 132374672 | solution.py:379
  816.8 20.4 dynamic_update_slice.9
  900.3 305.0 %reduce-scatter.31.cloned.1.call-done = bf16[128,2048]{1,0:T(8,128)(2,1)} async-done(((bf16[2048,2048]{1,0:T(8,128)(2,1)}), bf16[128,2048]{1,0:T(8,128)(2,1)}) %reduce-scatter.31.cloned.1.call-update) | async-done | bytes 524304
  1210.6 70.2 %reduce-scatter.33.cloned.1.call-done = bf16[128,2048]{1,0:T(8,128)(2,1)} async-done(((bf16[2048,2048]{1,0:T(8,128)(2,1)}), bf16[128,2048]{1,0:T(8,128)(2,1)}) %reduce-scatter.33.cloned.1.call-update) | async-done | bytes 524304
  1286.1 25.6 all_gather.106
  1311.7 33.2 %all_gather.107 = bf16[8,16,2048]{2,1,0:T(8,128)(2,1)S(1)} all-gather(bf16[1,16,2048]{2,1,0:T(8,128)(2,1)S(1)} %copy-done.29), channel_id=1, replica_groups=mesh['ctx'=16,'wsh'=8] {'wsh'}, dimensions={0}, use_global_device_ids=true | all-gather | bytes 589824 | tf_op jit(solution)/shard_map/all_gather | solution.py:141
  1344.9 31.7 %all_gather.112 = bf16[8,16,2048]{2,1,0:T(8,128)(2,1)S(1)} all-gather(bf16[1,16,2048]{2,1,0:T(8,128)(2,1)S(1)} %copy-done.30), channel_id=1, replica_groups=mesh['ctx'=16,'wsh'=8] {'wsh'}, dimensions={0}, use_global_device_ids=true | all-gather | bytes 589824 | tf_op jit(solution)/shard_map/all_gather | solution.py:144
  1378.7 256.2 %all-gather.40.cloned.1.call-done = bf16[8192,2048]{1,0:T(8,128)(2,1)} async-done(((bf16[1024,2048]{1,0:T(8,128)(2,1)}), bf16[8192,2048]{1,0:T(8,128)(2,1)}) %all-gather.40.cloned.1.call-update) | async-done | bytes 33554448 | tf_op jit(solution)/shard_map/all_gather | solution.py:139
  1654.6 314.5 %all-gather.36.cloned.1.call-done = bf16[2048,8192]{1,0:T(8,128)(2,1)} async-done(((bf16[256,8192]{1,0:T(8,128)(2,1)}), bf16[2048,8192]{1,0:T(8,128)(2,1)}) %all-gather.36.cloned.1.call-update) | async-done | bytes 33554448 | tf_op jit(solution)/shard_map/all_gather | solution.py:137
  1986.2 37.0 %all-gather.38.cloned.1.call-done = bf16[8,16,8192]{2,1,0:T(8,128)(2,1)} async-done(((bf16[1,16,8192]{2,1,0:T(8,128)(2,1)}), bf16[8,16,8192]{2,1,0:T(8,128)(2,1)}) %all-gather.38.cloned.1.call-update) | async-done | bytes 2097168 | tf_op jit(solution)/shard_map/all_gather | solution.py:142
  2029.3 47.9 %all-gather.42.cloned.1.call-done = bf16[8,16,8192]{2,1,0:T(8,128)(2,1)} async-done(((bf16[1,16,8192]{2,1,0:T(8,128)(2,1)}), bf16[8,16,8192]{2,1,0:T(8,128)(2,1)}) %all-gather.42.cloned.1.call-update) | async-done | bytes 2097168 | tf_op jit(solution)/shard_map/all_gather | solution.py:143
  2191.4 35.6 %reduce-scatter.17.cloned.1.call-done = bf16[1,3,16,2048]{3,2,1,0:T(8,128)(2,1)} async-done(((bf16[8,3,16,2048]{3,2,1,0:T(8,128)(2,1)}), bf16[1,3,16,2048]{3,2,1,0:T(8,128)(2,1)}) %reduce-scatter.17.cloned.1.call-update) | async-done | bytes 196624 | tf_op jit(solution)/shard_map/reduce_scatter | solution.py:453
  2227.0 71.8 %reduce-scatter.19.cloned.1.call-done = bf16[1,16,2048]{2,1,0:T(8,128)(2,1)} async-done(((bf16[8,16,2048]{2,1,0:T(8,128)(2,1)}), bf16[1,16,2048]{2,1,0:T(8,128)(2,1)}) %reduce-scatter.19.cloned.1.call-update) | async-done | bytes 65552 | tf_op jit(solution)/shard_map/reduce_scatter | solution.py:461
  2298.8 73.1 %reduce-scatter.21.cloned.1.call-done = bf16[1,16,2048]{2,1,0:T(8,128)(2,1)} async-done(((bf16[8,16,2048]{2,1,0:T(8,128)(2,1)}), bf16[1,16,2048]{2,1,0:T(8,128)(2,1)}) %reduce-scatter.21.cloned.1.call-update) | async-done | bytes 65552 | tf_op jit(solution)/shard_map/reduce_scatter | solution.py:467
  2371.9 72.8 %reduce-scatter.23.cloned.1.call-done = bf16[1,16,2048]{2,1,0:T(8,128)(2,1)} async-done(((bf16[8,16,2048]{2,1,0:T(8,128)(2,1)}), bf16[1,16,2048]{2,1,0:T(8,128)(2,1)}) %reduce-scatter.23.cloned.1.call-update) | async-done | bytes 65552 | tf_op jit(solution)/shard_map/reduce_scatter | solution.py:473
  2444.7 73.7 %reduce-scatter.29.cloned.1.call-done = bf16[1,16,2048]{2,1,0:T(8,128)(2,1)} async-done(((bf16[8,16,2048]{2,1,0:T(8,128)(2,1)}), bf16[1,16,2048]{2,1,0:T(8,128)(2,1)}) %reduce-scatter.29.cloned.1.call-update) | async-done | bytes 65552 | tf_op jit(solution)/shard_map/reduce_scatter | solution.py:491
  2518.4 78.2 %reduce-scatter.25.cloned.1.call-done = bf16[1,16,8192]{2,1,0:T(8,128)(2,1)} async-done(((bf16[8,16,8192]{2,1,0:T(8,128)(2,1)}), bf16[1,16,8192]{2,1,0:T(8,128)(2,1)}) %reduce-scatter.25.cloned.1.call-update) | async-done | bytes 262160 | tf_op jit(solution)/shard_map/reduce_scatter | solution.py:479
  2596.6 77.5 %reduce-scatter.27.cloned.1.call-done = bf16[1,16,8192]{2,1,0:T(8,128)(2,1)} async-done(((bf16[8,16,8192]{2,1,0:T(8,128)(2,1)}), bf16[1,16,8192]{2,1,0:T(8,128)(2,1)}) %reduce-scatter.27.cloned.1.call-update) | async-done | bytes 262160 | tf_op jit(solution)/shard_map/reduce_scatter | solution.py:485
  2678.4 120.0 %all-reduce.3.cloned.1.call-done = (bf16[1,3,16,2048]{3,2,1,0:T(8,128)(2,1)}, bf16[1,3,16,2048]{3,2,1,0:T(8,128)(2,1)}, bf16[1,16,2048]{2,1,0:T(8,128)(2,1)}, bf...) async-done(((bf16[1,3,16,2048]{3,2,1,0:T(8,128)(2,1)}, ...) | async-done | bytes 1179664 | tf_op jit(solution)/shard_map/psum | solution.py:499
  (337 shorter events, 482.7 us)
Async XLA Ops:
  7.2 75.0 %all-gather.22.cloned.1.call-start = ((), (), s32[]{:S(2)}) async-start(), calls=%async_computation.11 | async-start | bytes 1769472 | tf_op jit(solution)/shard_map/all_gather | solution.py:131
  8.0 163.0 %all-gather.20.cloned.1.call-start = ((), (), s32[]{:S(2)}) async-start(), calls=%async_computation.10 | async-start | bytes 9437184 | tf_op jit(solution)/shard_map/all_gather | solution.py:124
  8.7 211.8 %all-gather.24.cloned.1.call-start = ((), (), s32[]{:S(2)}) async-start(), calls=%async_computation.12 | async-start | bytes 1769472 | tf_op jit(solution)/shard_map/all_gather | solution.py:132
  9.4 319.2 %all-gather.28.cloned.1.call-start = ((), (), s32[]{:S(2)}) async-start(), calls=%async_computation.14 | async-start | bytes 9437184 | tf_op jit(solution)/shard_map/all_gather | solution.py:123
  10.0 425.8 %all-gather.30.cloned.1.call-start = ((), (), s32[]{:S(2)}) async-start(), calls=%async_computation.15 | async-start | bytes 9437184 | tf_op jit(solution)/shard_map/all_gather | solution.py:125
  10.6 545.8 %all-gather.34.cloned.1.call-start = ((), (), s32[]{:S(2)}) async-start(), calls=%async_computation.17 | async-start | bytes 9437184 | tf_op jit(solution)/shard_map/all_gather | solution.py:126
  11.2 606.7 %all-gather.26.cloned.1.call-start = ((), (), s32[]{:S(2)}) async-start(), calls=%async_computation.13 | async-start | bytes 8912896 | tf_op jit(solution)/shard_map/all_gather | solution.py:218
  82.2 353.7 %copy-start.2 = (bf16[128,2048]{1,0:T(8,128)(2,1)}, bf16[128,2048]{1,0:T(8,128)(2,1)S(1)}, u32[]{:S(2)}) copy-start(bf16[128,2048]{1,0:T(8,128)(2,1)S(1)} %fusion.82) | copy-start | bytes 1572868
  339.1 332.8 %all-gather.32.cloned.1.call-start = ((), (), s32[]{:S(2)}) async-start(), calls=%async_computation.16 | async-start | bytes 8912896 | tf_op jit(solution)/shard_map/all_gather | solution.py:219
  442.6 762.7 %reduce-scatter.31.cloned.1.call-start = ((), (), s32[]{:S(2)}) async-start(), calls=%async_computation.30 | async-start | bytes 8912896
  875.8 405.0 %reduce-scatter.33.cloned.1.call-start = ((), (), s32[]{:S(2)}) async-start(), calls=%async_computation.31 | async-start | bytes 8912896
  897.3 737.6 %all-gather.40.cloned.1.call-start = ((), (), s32[]{:S(2)}) async-start(), calls=%async_computation.20 | async-start | bytes 37748736 | tf_op jit(solution)/shard_map/all_gather | solution.py:139
  898.0 308.7 %copy-start.26 = (f32[128,16]{0,1:T(8,128)S(1)}, f32[128,16]{0,1:T(8,128)}, u32[]{:S(2)}) copy-start(f32[128,16]{0,1:T(8,128)} %copy-done.25) | copy-start | bytes 24580
  898.1 308.7 %copy-start.40 = (f32[128,16]{0,1:T(8,128)S(1)}, f32[128,16]{0,1:T(8,128)}, u32[]{:S(2)}) copy-start(f32[128,16]{0,1:T(8,128)} %get-tuple-element.501) | copy-start | bytes 24580
  898.1 1071.0 %all-gather.36.cloned.1.call-start = ((), (), s32[]{:S(2)}) async-start(), calls=%async_computation.18 | async-start | bytes 37748736 | tf_op jit(solution)/shard_map/all_gather | solution.py:137
  898.6 308.5 %copy-start.35 = (bf16[128,16]{0,1:T(8,128)(2,1)S(1)}, bf16[128,16]{0,1:T(8,128)(2,1)}, u32[]{:S(2)}) copy-start(bf16[128,16]{0,1:T(8,128)(2,1)} %copy-done.34) | copy-start | bytes 12292
  898.7 1124.5 %all-gather.38.cloned.1.call-start = ((), (), s32[]{:S(2)}) async-start(), calls=%async_computation.19 | async-start | bytes 2359296 | tf_op jit(solution)/shard_map/all_gather | solution.py:142
  899.4 1177.8 %all-gather.42.cloned.1.call-start = ((), (), s32[]{:S(2)}) async-start(), calls=%async_computation.21 | async-start | bytes 2359296 | tf_op jit(solution)/shard_map/all_gather | solution.py:143
  900.0 1291.4 %reduce-scatter.15.cloned.1.call-start = ((), (), s32[]{:S(2)}) async-start(), calls=%async_computation.22 | async-start | bytes 1769472 | tf_op jit(solution)/shard_map/reduce_scatter | solution.py:445
  900.2 308.7 %copy-start.3 = (bf16[128,2048]{1,0:T(8,128)(2,1)S(1)}, bf16[128,2048]{1,0:T(8,128)(2,1)}, u32[]{:S(2)}) copy-start(bf16[128,2048]{1,0:T(8,128)(2,1)} %copy-done.2) | copy-start | bytes 1572868
  900.3 308.8 %copy-start.33 = (bf16[128,16]{0,1:T(8,128)(2,1)S(1)}, bf16[128,16]{0,1:T(8,128)(2,1)}, u32[]{:S(2)}) copy-start(bf16[128,16]{0,1:T(8,128)(2,1)} %copy-done.32) | copy-start | bytes 12292
  1286.0 940.9 %reduce-scatter.17.cloned.1.call-start = ((), (), s32[]{:S(2)}) async-start(), calls=%async_computation.23 | async-start | bytes 1769472 | tf_op jit(solution)/shard_map/reduce_scatter | solution.py:453
  1378.6 920.1 %reduce-scatter.19.cloned.1.call-start = ((), (), s32[]{:S(2)}) async-start(), calls=%async_computation.24 | async-start | bytes 589824 | tf_op jit(solution)/shard_map/reduce_scatter | solution.py:461
  2088.9 283.0 %reduce-scatter.21.cloned.1.call-start = ((), (), s32[]{:S(2)}) async-start(), calls=%async_computation.25 | async-start | bytes 589824 | tf_op jit(solution)/shard_map/reduce_scatter | solution.py:467
  2089.5 355.2 %reduce-scatter.23.cloned.1.call-start = ((), (), s32[]{:S(2)}) async-start(), calls=%async_computation.26 | async-start | bytes 589824 | tf_op jit(solution)/shard_map/reduce_scatter | solution.py:473
  2090.2 428.2 %reduce-scatter.29.cloned.1.call-start = ((), (), s32[]{:S(2)}) async-start(), calls=%async_computation.29 | async-start | bytes 589824 | tf_op jit(solution)/shard_map/reduce_scatter | solution.py:491
  2093.7 502.9 %reduce-scatter.25.cloned.1.call-start = ((), (), s32[]{:S(2)}) async-start(), calls=%async_computation.27 | async-start | bytes 2359296 | tf_op jit(solution)/shard_map/reduce_scatter | solution.py:479
  2097.5 576.6 %reduce-scatter.27.cloned.1.call-start = ((), (), s32[]{:S(2)}) async-start(), calls=%async_computation.28 | async-start | bytes 2359296 | tf_op jit(solution)/shard_map/reduce_scatter | solution.py:485
  2158.1 640.4 %all-reduce.3.cloned.1.call-start = ((), (), s32[]{:S(2)}) async-start(), calls=%async_computation.32 | async-start | bytes 2359296 | tf_op jit(solution)/shard_map/psum | solution.py:499
  2177.1 499.7 %copy-start.47 = (f32[128]{0:T(128)S(1)}, f32[128]{0:T(128)}, u32[]{:S(2)}) copy-start(f32[128]{0:T(128)} %copy-done.46) | copy-start | bytes 1540
  2177.1 499.7 %copy-start.44 = (f32[128]{0:T(128)S(1)}, f32[128]{0:T(128)}, u32[]{:S(2)}) copy-start(f32[128]{0:T(128)} %copy-done.43) | copy-start | bytes 1540
  2191.4 485.4 %copy-start.12 = (f32[128,2048]{1,0:T(8,128)S(1)}, f32[128,2048]{1,0:T(8,128)}, u32[]{:S(2)}) copy-start(f32[128,2048]{1,0:T(8,128)} %get-tuple-element.515) | copy-start | bytes 3145732
  (48 other events, 2508.0 us)
Sparse Core Ops, SparseCore 0:
  10.4 52.2 all-gather.21
  65.0 105.8 all-gather.19
  173.2 47.2 all-gather.23
  222.8 105.8 all-gather.27
  330.8 105.0 all-gather.29
  438.1 118.3 all-gather.33
  558.6 59.2 all-gather.25
  620.2 51.6 all-gather.31
  875.9 329.3 reduce-scatter.30
  1207.5 73.1 reduce-scatter.32
  1283.1 351.7 all-gather.39
  1637.1 331.8 all-gather.35
  1971.4 51.7 all-gather.37
  2025.4 51.7 all-gather.41
  2080.7 70.1 reduce-scatter.14
  2155.0 71.9 reduce-scatter.16
  2230.3 68.3 reduce-scatter.18
  2302.6 69.2 reduce-scatter.20
  2375.4 69.2 reduce-scatter.22
  2449.1 69.2 reduce-scatter.28
  2522.2 74.3 reduce-scatter.24
  2600.3 73.7 reduce-scatter.26
  2677.2 121.2 all-reduce.2
where the time goes:
time: 2830 us; the launch traced here: 2820 us
  waiting for transfers between devices  2090 us (74%)
  blocking collectives  270 us (10%)
  matrix products  194 us (7%)
  local copies, waits for them, and re-layouts  169 us (6%)
  other arithmetic  48.7 us (2%)
  loops' own time  30.7 us (1%)
    unnamed x25, waiting for transfers between devices  383 us
    all_gather x1, waiting for transfers between devices, local(): lax.all_gather(feedforward_in_weight, 'wsh', axis=0, tiled=True)  314 us
    all_gather x1, waiting for transfers between devices, local(): lax.all_gather(feedforward_out_weight, 'wsh', axis=0, tiled=True)  256 us
    psum x1, waiting for transfers between devices, local(): lax.psum(shares[0].astype(jnp.bfloat16), 'ctx').astype(jnp.float32)  120 us
    all_gather x1, waiting for transfers between devices, local(): lax.all_gather(query_weight, 'wsh', axis=0, tiled=True)  103 us
    all_gather x1, waiting for transfers between devices, local(): lax.all_gather(key_weight, 'wsh', axis=0, tiled=True)  86.4 us
    all_gather x1, waiting for transfers between devices, local(): lax.all_gather(value_weight, 'wsh', axis=0, tiled=True)  80.3 us
    reduce_scatter x1, waiting for transfers between devices, local(): lax.psum_scatter(spread_out(feedforward_in_up_gradient).astype(jnp.bfloat...  78.2 us
  transfers between devices with their start and end apart: 23, of which 21 were waited for; matrix products, arithmetic and copies ran while one was open for 8% of the time, Pallas kernels for 0%

commit v1 on v0

v1 whole, which is shorter than its diff:
```python
import functools

import jax
import jax.numpy as jnp
import numpy as np
from jax import lax
from jax.experimental import pallas as pl
from jax.experimental.pallas import tpu as pltpu
from jax.sharding import Mesh, PartitionSpec as P

ADAPTERS = 8
RANK = 16
EPSILON = 1e-05
GELU_SCALE = 0.7978845608028654
NEGATIVE = -1e30
SCALE = 64 ** -0.5
BF = jnp.bfloat16
F32 = jnp.float32
WSH = ("y", "xh")
TP = ("xl", "z")
CTX = ("xl", "z", "c")
VMEM_LIMIT = 58 * 1024 * 1024


def nn(a, b):
    return lax.dot_general(a, b, (((1,), (0,)), ((), ())), preferred_element_type=F32)


def nt(a, b):
    return lax.dot_general(a, b, (((1,), (1,)), ((), ())), preferred_element_type=F32)


def tn(a, b):
    return lax.dot_general(a, b, (((0,), (0,)), ((), ())), preferred_element_type=F32)


def adapter_mask(aid, columns):
    col = lax.broadcasted_iota(jnp.int32, (aid.shape[0], columns), 1)
    return (lax.shift_right_logical(col, 4) & 7) == aid.astype(jnp.int32)


def turn(values, cosine, sine):
    width = values.shape[1]
    lane = lax.broadcasted_iota(jnp.int32, values.shape, 1) & 63
    partner = jnp.where(
        lane < 16, pltpu.roll(values, width - 16, 1), pltpu.roll(values, 16, 1)
    )
    return values * cosine + partner * sine


def k1_body(x_ref, wqkv_ref, down_ref, up_ref, misc_ref, bias_ref, cos_ref, sin_ref, hb_ref, inner_ref, qkv_ref):
    x = x_ref[:, :2048].astype(F32)
    aid = x_ref[:, 2048:2049].astype(F32)
    mean = jnp.mean(x, axis=1, keepdims=True)
    center = x - mean
    spread = jnp.mean(center * center, axis=1, keepdims=True)
    h = center * lax.rsqrt(spread + EPSILON) * misc_ref[0:1, :] + misc_ref[1:2, :]
    hb = h.astype(BF)
    hb_ref[...] = hb
    inner = nt(hb, down_ref[...])
    inner = jnp.where(adapter_mask(aid, 512), inner, 0.0).astype(BF)
    inner_ref[...] = inner
    cosine = jnp.concatenate([cos_ref[...]] * 2, axis=1)
    sine = jnp.concatenate([sin_ref[...]] * 2, axis=1)
    for p in range(3):
        cols = slice(256 * p, 256 * p + 256)
        pre = nn(hb, wqkv_ref[:, cols]) + nn(inner[:, 128 * p : 128 * p + 128], up_ref[:, cols])
        pre = pre + bias_ref[:, cols]
        if p < 2:
            pre = turn(pre, cosine, sine)
        low = pre.astype(BF)
        qkv_ref[0, p] = low[:, :128]
        qkv_ref[1, p] = low[:, 128:]


def whole(shape):
    return pl.BlockSpec(shape, lambda t: (0,) * len(shape))


def k1(xg, wqkv, downs, ups, misc, bias, cosine, sine):
    rows = 256
    return pl.pallas_call(
        k1_body,
        grid=(1024 // rows,),
        in_specs=[
            pl.BlockSpec((rows, 2176), lambda t: (t, 0)),
            whole((2048, 768)),
            whole((512, 2048)),
            whole((128, 768)),
            whole((2, 2048)),
            whole((1, 768)),
            pl.BlockSpec((rows, 128), lambda t: (t, 0)),
            pl.BlockSpec((rows, 128), lambda t: (t, 0)),
        ],
        out_specs=[
            pl.BlockSpec((rows, 2048), lambda t: (t, 0)),
            pl.BlockSpec((rows, 512), lambda t: (t, 0)),
            pl.BlockSpec((2, 3, rows, 128), lambda t: (0, 0, t, 0)),
        ],
        out_shape=[
            jax.ShapeDtypeStruct((1024, 2048), BF),
            jax.ShapeDtypeStruct((1024, 512), BF),
            jax.ShapeDtypeStruct((2, 3, 1024, 128), BF),
        ],
        compiler_params=pltpu.CompilerParams(vmem_limit_bytes=VMEM_LIMIT),
        name="norm_qkv",
    )(xg, wqkv, downs, ups, misc, bias, cosine, sine)


def k1b_body(dy_ref, aid_ref, wd_ref, ud_ref, dd_ref, dob_ref, ginner_ref):
    dy = dy_ref[...]
    aid = aid_ref[:, 0:1].astype(F32)
    ginner = jnp.where(adapter_mask(aid, 128), nt(dy, ud_ref[...]), 0.0).astype(BF)
    ginner_ref[...] = ginner
    dob = (nt(dy, wd_ref[...]) + nn(ginner, dd_ref[...])).astype(BF)
    dob_ref[0] = dob[:, :128]
    dob_ref[1] = dob[:, 128:]


def k1b(dyg, aid, wd, ud, dd):
    rows = 256
    return pl.pallas_call(
        k1b_body,
        grid=(1024 // rows,),
        in_specs=[
            pl.BlockSpec((rows, 2048), lambda t: (t, 0)),
            pl.BlockSpec((rows, 128), lambda t: (t, 0)),
            whole((256, 2048)),
            whole((128, 2048)),
            whole((128, 256)),
        ],
        out_specs=[
            pl.BlockSpec((2, rows, 128), lambda t: (0, t, 0)),
            pl.BlockSpec((rows, 128), lambda t: (t, 0)),
        ],
        out_shape=[
            jax.ShapeDtypeStruct((2, 1024, 128), BF),
            jax.ShapeDtypeStruct((1024, 128), BF),
        ],
        compiler_params=pltpu.CompilerParams(vmem_limit_bytes=VMEM_LIMIT),
        name="attention_output_grad",
    )(dyg, aid, wd, ud, dd)


def k3_body(qkvd_ref, idrow_ref, idcol_ref, cos_ref, sin_ref, out_ref, kt_s, vt_s, dk_s, dv_s):
    kt_s[...] = qkvd_ref[1].T
    vt_s[...] = qkvd_ref[2].T
    dk_s[...] = jnp.zeros_like(dk_s)
    dv_s[...] = jnp.zeros_like(dv_s)
    tile = 256
    lane = lax.broadcasted_iota(jnp.int32, (tile, 128), 1)
    for t in range(8):
        rows = slice(tile * t, tile * t + tile)
        length = min(tile * (t + 2), 2048)
        free = tile * t
        q = qkvd_ref[0, rows]
        dob = qkvd_ref[3, rows]
        query_ids = idrow_ref[0:1, rows]
        allowed = idcol_ref[free:length, 0:1] <= query_ids
        o_parts, dq_parts = [], []
        for h in range(2):
            mine = (lane >= 64 * h) & (lane < 64 * h + 64)
            qh = jnp.where(mine, q, jnp.zeros_like(q))
            dh = jnp.where(mine, dob, jnp.zeros_like(dob))
            s_tail = jnp.where(allowed, nt(qkvd_ref[1, free:length], qh), NEGATIVE)
            largest = jnp.max(s_tail, axis=0, keepdims=True)
            if free:
                s_head = nt(qkvd_ref[1, :free], qh)
                largest = jnp.maximum(largest, jnp.max(s_head, axis=0, keepdims=True))
                s = jnp.concatenate([s_head, s_tail], axis=0)
            else:
                s = s_tail
            e = jnp.exp((s - largest) * SCALE)
            recip = 1.0 / jnp.sum(e, axis=0, keepdims=True)
            p = e * recip
            pb = p.astype(BF)
            ot = nn(vt_s[64 * h : 64 * h + 64, :length], pb)
            dp = nt(qkvd_ref[2, :length], dh)
            delta = jnp.sum(p * dp, axis=0, keepdims=True)
            ds = (p * (dp - delta)).astype(BF)
            dqt = nn(kt_s[64 * h : 64 * h + 64, :length], ds)
            dk_s[:length] += nn(ds, qh)
            dv_s[:length] += nn(pb, dh)
            o_parts.append(ot)
            dq_parts.append(dqt)
        o = jnp.concatenate(o_parts, axis=0).T
        dq = jnp.concatenate(dq_parts, axis=0).T * SCALE
        out_ref[0, rows] = o.astype(BF)
        out_ref[1, rows] = turn(dq, cos_ref[rows], -sin_ref[rows]).astype(BF)
    out_ref[2] = turn(dk_s[...] * SCALE, cos_ref[...], -sin_ref[...]).astype(BF)
    out_ref[3] = dv_s[...].astype(BF)


def k3(qkvd, idrow, idcol, cosine, sine):
    return pl.pallas_call(
        k3_body,
        out_shape=jax.ShapeDtypeStruct((4, 2048, 128), BF),
        scratch_shapes=[
            pltpu.VMEM((128, 2048), BF),
            pltpu.VMEM((128, 2048), BF),
            pltpu.VMEM((2048, 128), F32),
            pltpu.VMEM((2048, 128), F32),
        ],
        compiler_params=pltpu.CompilerParams(vmem_limit_bytes=VMEM_LIMIT),
        name="attention",
    )(qkvd, idrow, idcol, cosine, sine)


def k2_body(
    hb_ref, dy_ref, aid_ref, inner_ref, gdense_ref, att_ref,
    w1_ref, w2_ref, wd_ref, wqkv_ref, down_ref, up_ref, up1_ref, d2_ref, u2_ref, ud_ref, dd_ref, b1_ref, fold_ref,
    out_ref, dh_ref, small_ref, gup1_ref, gd2_ref, gqkv_ref, gdd_ref,
):
    step = pl.program_id(0)
    hb = hb_ref[...]
    dy = dy_ref[...]
    aid = aid_ref[:, 0:1].astype(F32)
    keep = adapter_mask(aid, 128)
    inner = inner_ref[...]

    def masked(v):
        return jnp.where(keep, v, 0.0).astype(BF)

    f = nn(hb, w1_ref[...]) + nn(inner[:, 384:512], up1_ref[...]) + b1_ref[...]
    square = f * f
    th = jnp.tanh(GELU_SCALE * f * (1.0 + 0.044715 * square))
    half = 0.5 * (1.0 + th)
    gb = (f * half).astype(BF)
    slope = half + 0.5 * f * (1.0 - th * th) * GELU_SCALE * (1.0 + 3 * 0.044715 * square)
    ob = att_ref[0]
    inner2 = masked(nt(gb, d2_ref[...]))
    innerd = masked(nt(ob, dd_ref[...]))
    out = nn(gb, w2_ref[...]) + nn(inner2, u2_ref[...]) + nn(ob, wd_ref[...]) + nn(innerd, ud_ref[...])
    out_ref[...] = out.astype(BF)
    ginner2 = masked(nt(dy, u2_ref[...]))
    dg = nt(dy, w2_ref[...]) + nn(ginner2, d2_ref[...])
    df = (dg * slope).astype(BF)
    ginner1 = masked(nt(df, up1_ref[...]))
    dh = nt(df, w1_ref[...])
    small = []
    gqkv = []
    for p in range(3):
        cols = slice(256 * p, 256 * p + 256)
        dpre = att_ref[p + 1]
        ginner = masked(nt(dpre, up_ref[:, cols]))
        small.append(ginner)
        dh = dh + nt(dpre, wqkv_ref[:, cols])
        gqkv.append(tn(inner[:, 128 * p : 128 * p + 128], dpre))
    small.append(ginner1)
    dh = dh + nn(jnp.concatenate(small, axis=1), down_ref[...])
    dh_ref[...] = dh.astype(BF)
    small = jnp.concatenate(small + [innerd, inner2], axis=1)
    small_ref[...] = nn(small, fold_ref[...]).astype(BF)
    gup1 = tn(inner[:, 384:512], df)
    gd2 = tn(ginner2, gb)
    gdd = tn(gdense_ref[...], ob)
    gqkv = jnp.concatenate(gqkv, axis=1)

    @pl.when(step == 0)
    def _():
        gup1_ref[...] = gup1
        gd2_ref[...] = gd2
        gdd_ref[...] = gdd
        gqkv_ref[...] = gqkv

    @pl.when(step > 0)
    def _():
        gup1_ref[...] += gup1
        gd2_ref[...] += gd2
        gdd_ref[...] += gdd
        gqkv_ref[...] += gqkv


def k2(hb, dyg, aid, inner, gdense, att, w1, w2, wd, wqkv, downs, ups, up1, d2, u2, ud, dd, b1, fold):
    rows = 256

    def once(shape):
        return pl.BlockSpec(shape, lambda t: (0,) * len(shape), pipeline_mode=pl.Buffered(1))

    return pl.pallas_call(
        k2_body,
        grid=(1024 // rows,),
        in_specs=[
            pl.BlockSpec((rows, 2048), lambda t: (t, 0)),
            pl.BlockSpec((rows, 2048), lambda t: (t, 0)),
            pl.BlockSpec((rows, 128), lambda t: (t, 0)),
            pl.BlockSpec((rows, 512), lambda t: (t, 0)),
            pl.BlockSpec((rows, 128), lambda t: (t, 0)),
            pl.BlockSpec((4, rows, 256), lambda t: (0, t, 0)),
            once((2048, 1024)),
            once((1024, 2048)),
            once((256, 2048)),
            once((2048, 768)),
            once((512, 2048)),
            once((128, 768)),
            once((128, 1024)),
            once((128, 1024)),
            once((128, 2048)),
            once((128, 2048)),
            once((128, 256)),
            once((1, 1024)),
            once((768, 128)),
        ],
        out_specs=[
            pl.BlockSpec((rows, 2048), lambda t: (t, 0)),
            pl.BlockSpec((rows, 2048), lambda t: (t, 0)),
            pl.BlockSpec((rows, 128), lambda t: (t, 0)),
            whole((128, 1024)),
            whole((128, 1024)),
            whole((128, 768)),
            whole((128, 256)),
        ],
        out_shape=[
            jax.ShapeDtypeStruct((1024, 2048), BF),
            jax.ShapeDtypeStruct((1024, 2048), BF),
            jax.ShapeDtypeStruct((1024, 128), BF),
            jax.ShapeDtypeStruct((128, 1024), F32),
            jax.ShapeDtypeStruct((128, 1024), F32),
            jax.ShapeDtypeStruct((128, 768), F32),
            jax.ShapeDtypeStruct((128, 256), F32),
        ],
        compiler_params=pltpu.CompilerParams(vmem_limit_bytes=VMEM_LIMIT),
        name="feed_forward_both_ways",
    )(hb, dyg, aid, inner, gdense, att, w1, w2, wd, wqkv, downs, ups, up1, d2, u2, ud, dd, b1, fold)


def k5_body(small_ref, aid_ref, hb_ref, dy_ref, spread_ref, gdown_ref, gup_ref):
    aid = aid_ref[:, 0:1].astype(F32)
    wide = jnp.where(adapter_mask(aid, 768), nn(small_ref[...], spread_ref[...]), 0.0).astype(BF)
    gdown_ref[...] = tn(wide[:, :512], hb_ref[...])
    gup_ref[...] = tn(wide[:, 512:], dy_ref[...])


def k5(small, aid, hb_cols, dy_cols, spread):
    return pl.pallas_call(
        k5_body,
        out_shape=[
            jax.ShapeDtypeStruct((512, 256), F32),
            jax.ShapeDtypeStruct((256, 256), F32),
        ],
        compiler_params=pltpu.CompilerParams(vmem_limit_bytes=VMEM_LIMIT),
        name="adapter_grads",
    )(small, aid, hb_cols, dy_cols, spread)


def rotary_tables():
    lane = np.arange(128) % 64
    rate = np.where(lane < 32, 10000.0 ** (-2.0 * (lane % 16) / 32.0), 0.0).astype(np.float32)
    sign = np.where(lane < 16, -1.0, 1.0).astype(np.float32)
    angles = jnp.arange(2048, dtype=jnp.int32).astype(F32)[:, None] * jnp.asarray(rate)[None, :]
    return jnp.cos(angles), jnp.sin(angles) * jnp.asarray(sign)[None, :]


def fold_matrix():
    row = np.arange(768)
    target = (row // 128) * 16 + row % 16
    return jnp.asarray((target[:, None] == np.arange(128)[None, :]).astype(np.float32)).astype(BF)


def halves(a):
    m = a.shape[1] // 2
    return jnp.concatenate([a[:, :m], a[:, m:]], axis=0)


def gather_pair(own, single):
    xh = lax.axis_index("xh")
    other = lax.ppermute(own, "xh", [(0, 1), (1, 0)])
    first = jnp.where(xh == 0, own, other)
    second = jnp.where(xh == 0, other, own)
    parts = [first, second]
    if single is not None:
        parts.append(single)
    packed = jnp.concatenate(parts, axis=0)
    rows = own.shape[0]
    g = lax.all_gather(packed, ("y", "c"), axis=0, tiled=False)
    g = g.reshape((4, 2) + packed.shape)
    main = g[:, :, : 2 * rows].reshape(4, 2, 2, rows, packed.shape[1])
    main = main.transpose(0, 2, 1, 3, 4).reshape(8, 2, rows, packed.shape[1])
    return main, g[:, :, 2 * rows :]


def local(
    inputs,
    output_cotangent,
    block_index_per_position,
    adapter_index_per_run,
    norm_gain,
    norm_bias,
    query_weight,
    key_weight,
    value_weight,
    dense_weight,
    query_bias,
    key_bias,
    value_bias,
    dense_bias,
    feedforward_in_weight,
    feedforward_in_bias,
    feedforward_out_weight,
    feedforward_out_bias,
    adapter_attention_down,
    adapter_attention_up,
    adapter_dense_down,
    adapter_dense_up,
    adapter_feedforward_in_down,
    adapter_feedforward_in_up,
    adapter_feedforward_out_down,
    adapter_feedforward_out_up,
):
    xl, z, c = lax.axis_index("xl"), lax.axis_index("z"), lax.axis_index("c")
    xh = lax.axis_index("xh")
    j = xl * 4 + z
    x_own = inputs[0]
    dy_own = output_cotangent[0]
    run_adapter = adapter_index_per_run[0, 0].astype(F32).astype(BF)
    block_row = block_index_per_position[0]

    def row_half(a):
        n = a.shape[0] // 2
        return lax.dynamic_slice_in_dim(a, c * n, n, 0)

    def col_half(a):
        n = a.shape[1] // 2
        return lax.dynamic_slice_in_dim(a, c * n, n, 1)

    def head_cols(a):
        return jnp.concatenate(
            [lax.dynamic_slice_in_dim(a, (2 * i + xl) * 256 + z * 64, 64, 1) for i in range(4)], axis=1
        )

    def hidden_cols(a):
        return jnp.concatenate(
            [lax.dynamic_slice_in_dim(a, 1024 * w + 128 * j, 128, 1) for w in range(8)], axis=1
        )

    qkv_half = jnp.concatenate(
        [head_cols(row_half(a)) for a in (query_weight, key_weight, value_weight)], axis=1
    )
    downs_own = jnp.concatenate([adapter_attention_down[0].reshape(48, 2048), adapter_feedforward_in_down[0]], axis=0)
    downs_half = row_half(downs_own)
    side = jnp.concatenate([downs_half[:16, 256 * b : 256 * b + 256] for b in range(8)], axis=0)
    ups16 = jnp.concatenate(
        [head_cols(adapter_attention_up[0, p]) for p in range(3)] + [head_cols(adapter_dense_down[0])], axis=1
    )

    def head_bias(a):
        return lax.dynamic_slice_in_dim(a, z * 64, 64, 0)

    row0 = jnp.concatenate([norm_gain, norm_bias, dense_bias, feedforward_out_bias])
    row1 = jnp.concatenate(
        [
            head_bias(query_bias),
            head_bias(key_bias),
            head_bias(value_bias),
            jnp.zeros((64,), BF),
            lax.dynamic_slice_in_dim(feedforward_in_bias, 128 * j, 128, 0),
            jnp.zeros((640,), BF),
        ]
    )
    misc16 = jnp.concatenate([row0[None], row1[None], jnp.zeros((14, 1024), BF)], axis=0)
    own1 = jnp.concatenate(
        [
            jnp.concatenate([qkv_half, side], axis=1),
            halves(downs_half[16:32]),
            jnp.where(c == 0, ups16, misc16),
            col_half(adapter_dense_up[0]),
        ],
        axis=0,
    )
    dense_rows = row_half(lax.dynamic_slice_in_dim(dense_weight, 64 * z, 64, 0))
    dense_piece = halves(dense_rows)
    dense_other = lax.ppermute(dense_piece, "xh", [(0, 1), (1, 0)])
    dense_piece = jnp.where(xh == xl, dense_piece, dense_other)

    own2 = jnp.concatenate(
        [
            hidden_cols(row_half(feedforward_in_weight)),
            hidden_cols(jnp.where(c == 0, adapter_feedforward_in_up[0], adapter_feedforward_out_down[0])),
            halves(row_half(lax.dynamic_slice_in_dim(feedforward_out_weight, 128 * j, 128, 0))),
            col_half(adapter_feedforward_out_up[0]),
        ],
        axis=0,
    )

    x_send = jnp.concatenate([x_own, jnp.full((128, 128), run_adapter, BF)], axis=1)
    xg = lax.all_gather(x_send, TP, axis=0, tiled=True)
    g1, dense_g = gather_pair(own1, dense_piece)
    dyg = lax.all_gather(dy_own, TP, axis=0, tiled=True)
    g2, _ = gather_pair(own2, None)

    wqkv = g1[:, :, :128, :768].reshape(2048, 768)
    first = g1[:, :, :128, 768:].reshape(8, 2, 8, 16, 256).transpose(1, 0, 3, 2, 4).reshape(2, 1, 128, 2048)
    second = g1[:, :, 128:160].reshape(8, 2, 2, 16, 1024).transpose(1, 0, 3, 2, 4).reshape(2, 1, 128, 2048)
    downs = jnp.concatenate([first, second], axis=1).reshape(512, 2048)
    ups = g1[:, 0, 160:176, :768].reshape(128, 768)
    dd = g1[:, 0, 160:176, 768:].reshape(128, 256)
    misc = g1[:, 1, 160, :].reshape(8, 4, 256).transpose(1, 0, 2).reshape(4, 2048).astype(F32)
    rest = g1[:, 1, 161, :].astype(F32)
    head_b = lax.dynamic_index_in_dim(rest[:, :192].reshape(4, 2, 3, 64), xl, 1, keepdims=False)
    bias_qkv = head_b.transpose(1, 0, 2).reshape(1, 768)
    b1 = rest[:, 256:384].reshape(1, 1024)
    ud = g1[:, :, 176:192].transpose(0, 2, 1, 3).reshape(128, 2048)
    wd = dense_g.reshape(4, 2, 2, 32, 1024).transpose(0, 1, 3, 2, 4).reshape(256, 2048)
    w1 = g2[:, :, :128].reshape(2048, 1024)
    up1 = g2[:, 0, 128:144].reshape(128, 1024)
    d2 = g2[:, 1, 128:144].reshape(128, 1024)
    w2 = g2[:, :, 144:272].reshape(8, 2, 2, 64, 1024).transpose(0, 1, 3, 2, 4).reshape(1024, 2048)
    u2 = g2[:, :, 272:288].transpose(0, 2, 1, 3).reshape(128, 2048)

    cos_all, sin_all = rotary_tables()

    def my_tokens(a):
        return lax.dynamic_index_in_dim(a.reshape(8, 2, 128, 128), c, 1, keepdims=False).reshape(1024, 128)

    hb, inner, qkv2 = k1(xg, wqkv, downs, ups, misc[:2], bias_qkv, my_tokens(cos_all), my_tokens(sin_all))
    aid = xg[:, 2048:]
    dob2, gdense = k1b(dyg, aid, wd, ud, dd)

    swap = [(0, 1), (1, 0)]
    both = jnp.concatenate([qkv2, dob2[:, None]], axis=1)
    mine = lax.dynamic_index_in_dim(both, c, 0, keepdims=False)
    theirs = lax.ppermute(lax.dynamic_index_in_dim(both, 1 - c, 0, keepdims=False), "c", swap)
    even = jnp.where(c == 0, mine, theirs).reshape(4, 8, 1, 128, 128)
    odd = jnp.where(c == 0, theirs, mine).reshape(4, 8, 1, 128, 128)
    qkvd = jnp.concatenate([even, odd], axis=2).reshape(4, 2048, 128)
    idrow = jnp.broadcast_to(block_row[None, :], (8, 2048))
    idcol = jnp.broadcast_to(block_row[:, None], (2048, 128))
    att = k3(qkvd, idrow, idcol, cos_all, sin_all)
    att = att.reshape(4, 8, 2, 128, 128)
    mine = lax.dynamic_index_in_dim(att, c, 2, keepdims=False).reshape(4, 1024, 128)
    theirs = lax.ppermute(
        lax.dynamic_index_in_dim(att, 1 - c, 2, keepdims=False).reshape(4, 1024, 128), "c", swap
    )
    att = jnp.concatenate([jnp.where(c == 0, mine, theirs), jnp.where(c == 0, theirs, mine)], axis=2)

    fold = fold_matrix()
    out_part, dh_part, small, gup1, gd2, gqkv, gdd = k2(
        hb, dyg, aid, inner, gdense, att, w1, w2, wd, wqkv, downs, ups, up1, d2, u2, ud, dd, b1, fold
    )
    out_sum = lax.psum_scatter(out_part, TP, scatter_dimension=0, tiled=True)
    dh_sum = lax.psum_scatter(dh_part, TP, scatter_dimension=0, tiled=True)

    small = lax.all_to_all(small.reshape(8, 128, 128), TP, 0, 0, tiled=True)
    small = jnp.sum(small.astype(F32), axis=0).astype(BF)
    small = lax.all_to_all(jnp.broadcast_to(small[None], (8, 128, 128)), TP, 0, 0, tiled=True).reshape(1024, 128)
    hb_cols = lax.dynamic_slice_in_dim(hb, 256 * j, 256, 1)
    dy_cols = lax.dynamic_slice_in_dim(dyg, 256 * j, 256, 1)
    gdown, gup = k5(small, aid, hb_cols, dy_cols, fold.T)

    gdown = gdown.reshape(4, 8, 16, 256).transpose(1, 2, 0, 3).reshape(8, 16, 1024)
    gqkvd = jnp.concatenate([gqkv, gdd], axis=1).reshape(8, 16, 1024)
    gup = gup.reshape(2, 8, 16, 256).transpose(1, 2, 0, 3).reshape(8, 16, 512)
    gup = jnp.concatenate([gup, jnp.zeros_like(gup)], axis=2)
    grads = jnp.concatenate([gdown, gqkvd, gup1.reshape(8, 16, 1024), gd2.reshape(8, 16, 1024), gup], axis=1)
    keep = lax.dynamic_slice_in_dim(grads, 40 * c, 40, 1)
    send = lax.dynamic_slice_in_dim(grads, 40 * (1 - c), 40, 1).astype(BF)
    grads = (keep + lax.ppermute(send, "c", swap).astype(F32)).astype(BF)
    grads = lax.all_to_all(grads, WSH, 0, 0, tiled=True)
    grads = jnp.sum(grads.astype(F32), axis=0).astype(BF)
    grads = lax.all_to_all(jnp.broadcast_to(grads[None], (16, 40, 1024)), CTX, 0, 0, tiled=True)
    grads = grads.reshape(8, 80, 1024).astype(F32)

    def from_heads(a):
        return a.reshape(2, 4, 16, 4, 64).transpose(2, 3, 0, 1, 4).reshape(16, 2048)

    def from_blocks(a):
        return a.transpose(1, 0, 2).reshape(16, 2048)

    def from_hidden(a):
        return a.reshape(8, 16, 8, 128).transpose(1, 2, 0, 3).reshape(16, 8192)

    downs_g = [from_blocks(grads[:, :16, 256 * p : 256 * p + 256]) for p in range(4)]
    ups_g = [from_heads(grads[:, 16:32, 256 * p : 256 * p + 256]) for p in range(4)]
    gup1 = from_hidden(grads[:, 32:48])
    gd2 = from_hidden(grads[:, 48:64])
    gud = from_blocks(grads[:, 64:80, :256])
    gu2 = from_blocks(grads[:, 64:80, 256:512])

    source = x_own.astype(F32)
    outputs = (source + out_sum.astype(F32) + misc[2:3] + misc[3:4]).astype(BF)[None]
    mean = jnp.mean(source, axis=1, keepdims=True)
    center = source - mean
    inv = lax.rsqrt(jnp.mean(center * center, axis=1, keepdims=True) + EPSILON)
    hn = center * inv
    e = dh_sum.astype(F32) * misc[0:1]
    dx = (e - jnp.mean(e, axis=1, keepdims=True) - hn * jnp.mean(e * hn, axis=1, keepdims=True)) * inv
    grad_inputs = (dy_own.astype(F32) + dx).astype(BF)[None]
    return (
        outputs,
        grad_inputs,
        jnp.stack(downs_g[:3])[None],
        jnp.stack(ups_g[:3])[None],
        ups_g[3][None],
        gud[None],
        downs_g[3][None],
        gup1[None],
        gd2[None],
        gu2[None],
    )


def solution(mesh):
    fine = Mesh(np.asarray(mesh.devices).reshape(2, 4, 2, 4, 2), ("xl", "z", "c", "y", "xh"))
    tokens = P(WSH, CTX, None)
    w1 = P(WSH)
    w2 = P(WSH, None)
    w3 = P(WSH, None, None)
    w4 = P(WSH, None, None, None)
    placed = (tokens, tokens, w2, P(WSH, CTX)) + (w1, w1, w2, w2, w2, w2, w1, w1, w1, w1, w2, w1, w2, w1)
    placed = placed + (w4, w4, w3, w3, w3, w3, w3, w3)
    return jax.shard_map(
        local,
        mesh=fine,
        in_specs=placed,
        out_specs=(tokens, tokens, w4, w4, w3, w3, w3, w3, w3, w3),
        check_vma=False,
    )
```

time: 2830 us -> 504 us (0.18)
  waiting for transfers between devices: 2090 us -> 176 us
  blocking collectives: 270 us -> 18.9 us
  matrix products: 194 us -> 0 us
  Pallas kernels: 0 us -> 123 us
  local copies, waits for them, and re-layouts: 169 us -> 112 us
  loops' own time: 30.7 us -> 0 us
    all_gather x12 -> x4, waiting for transfers between devices: 1100 us -> 79.9 us  [the longest x2 43.6 us: gather_pair(): g = lax.all_gather(packed, ('y', 'c'), axis=0, tiled=False)]
    reduce_scatter x8 -> x2, waiting for transfers between devices: 483 us -> 0.02 us  [the longest x1 0.02 us: local(): out_sum = lax.psum_scatter(out_part, TP, scatter_dimension=0, tiled=True)]
    unnamed x25 -> x6, waiting for transfers between devices: 383 us -> 1.27 us
    all_gather x12 -> x0, blocking collectives: 270 us -> none  [the longest x1 33.2 us: local(): lax.all_gather(adapter_feedforward_in_down, 'wsh', axis=0, tiled=True)]
    dot_general x55 -> x0, matrix products: 194 us -> none  [the longest x18 70.2 us: contract_last(): lax.dot_general(left, right, (((1,), (1,)), ((), ())), preferred_element_...]
    pallas_call x0 -> x5, Pallas kernels: none -> 123 us  [the longest x1 59.1 us: k2(): pl.pallas_call(k2_body, grid=(1024 // rows,), in_specs=[pl.BlockSpec((row...]
    psum x1 -> x0, waiting for transfers between devices: 120 us -> none  [local(): lax.psum(shares[0].astype(jnp.bfloat16), 'ctx').astype(jnp.float32)]
    ppermute x0 -> x6, waiting for transfers between devices: none -> 50.6 us  [the longest x2 25.6 us: gather_pair(): other = lax.ppermute(own, 'xh', [(0, 1), (1, 0)])]
  transfers between devices with their start and end apart: 23 -> 15, of which waited for: 21 -> 10; matrix products, arithmetic and copies ran while one was open for 8% -> 21% of each run, Pallas kernels for 0% -> 13%
where the time goes in v1:
time: 504 us; the launch traced here: 499 us
  waiting for transfers between devices  176 us (35%)
  Pallas kernels  123 us (24%)
  local copies, waits for them, and re-layouts  112 us (22%)
  other arithmetic  29.5 us (6%)
  starting transfers between devices  22.8 us (5%)
  blocking collectives  18.9 us (4%)
  between operations  16.2 us (3%)
    pallas_call x1, Pallas kernels, k2(): pl.pallas_call(k2_body, grid=(1024 // rows,), in_specs=[pl.BlockSpec((row...  59.1 us
    all_gather x2, waiting for transfers between devices, gather_pair(): g = lax.all_gather(packed, ('y', 'c'), axis=0, tiled=False)  43.6 us
    pallas_call x1, Pallas kernels, k3(): pl.pallas_call(k3_body, out_shape=jax.ShapeDtypeStruct((4, 2048, 128), BF...  38.6 us
    all_gather x1, waiting for transfers between devices, local(): dyg = lax.all_gather(dy_own, TP, axis=0, tiled=True)  33.3 us
    all_to_all x1, waiting for transfers between devices, local(): lax.all_to_all(jnp.broadcast_to(grads[None], (16, 40, 1024)), CTX, 0, 0,...  30.2 us
    ppermute x2, waiting for transfers between devices, gather_pair(): other = lax.ppermute(own, 'xh', [(0, 1), (1, 0)])  25.6 us
    unnamed x113, local copies, waits for them, and re-layouts  23.1 us
    ppermute x1, waiting for transfers between devices, local(): dense_other = lax.ppermute(dense_piece, 'xh', [(0, 1), (1, 0)])  21.1 us
  transfers between devices with their start and end apart: 15, of which 10 were waited for; matrix products, arithmetic and copies ran while one was open for 21% of the time, Pallas kernels for 13%

profile of v1, /device:TPU:1, one launch (start us, length us, event | category | flops | bytes accessed | tf_op | source)
XLA Modules:
  0.0 499.2 jit_solution(6931072292808973427)
XLA Ops:
  8.0 1.9 concatenate.69
  18.0 3.7 collective-permute-start
  22.8 21.1 %collective-permute-done.1 = bf16[64,1024]{1,0:T(8,128)(2,1)S(1)} collective-permute-done((bf16[64,1024]{1,0:T(8,128)(2,1)S(1)}, bf16[64,1024]{1,0:T(8,128)(2,1)S(1)}, u32[]{:S(2)}, u32[]{:S(2)}) %collective-permute-start.1) | collective-permute-done | bytes 131104 | tf_op jit(solution)/shard_map/ppermute | solution.py:472
  55.8 3.9 collective-permute-start.4
  59.7 25.6 %collective-permute-done.4 = bf16[288,1024]{1,0:T(8,128)(2,1)S(1)} collective-permute-done((bf16[288,1024]{1,0:T(8,128)(2,1)S(1)}, bf16[288,1024]{1,0:T(8,128)(2,1)S(1)}, u32[]{:S(2)}, u32[]{:S(2)}) %collective-permute-start.4) | collective-permute-done | bytes 589856 | tf_op jit(solution)/shard_map/ppermute | solution.py:367
  87.1 2.7 sine_multiply_fusion
  89.7 2.9 all-gather.8.cloned.1.call-done.x_ref
  94.3 43.6 %all-gather.10.cloned.1.call-done = bf16[3584,1024]{1,0:T(8,128)(2,1)} async-done(((bf16[448,1024]{1,0:T(8,128)(2,1)}), bf16[3584,1024]{1,0:T(8,128)(2,1)}) %all-gather.10.cloned.1.call-update) | async-done | bytes 7340048 | tf_op jit(solution)/shard_map/all_gather | solution.py:375
  138.0 2.3 slice.242
  140.3 3.8 fusion.49
  145.6 2.5 slice.233
  158.8 33.3 %all-gather.12.cloned.1.call-done = bf16[1,1024,2048]{2,1,0:T(8,128)(2,1)} async-done(((bf16[1,128,2048]{2,1,0:T(8,128)(2,1)}), bf16[1,1024,2048]{2,1,0:T(8,128)(2,1)}) %all-gather.12.cloned.1.call-update) | async-done | bytes 4194320 | tf_op jit(solution)/shard_map/all_gather | solution.py:488
  192.1 7.8 %attention_output_grad.1 = (bf16[2,1024,128]{2,1,0:T(8,128)(2,1)}, bf16[1024,128]{1,0:T(8,128)(2,1)}) custom-call(bf16[1024,2048]{1,0:T(8,128)(2,1)} %bitcast.249, bf16[1024,128]{1,0:T(8,128)(2,1)} %slice.241.aid_ref, bf16[256,2048]{1,0:T(8,128)(2,1)} %bitcast.259, bf16[128,2048]{1,0:T(8,128)(2,1)} %bitcast.266, bf16[128,256]{1,0:T(8,128)(2,1)} %bitcast.298), custom_call_target="tpu_custom_call" | custom-call | tf_op jit(solution)/shard_map/attention_output_grad/pallas_call | solution.py:122
  201.4 14.5 %norm_qkv.1 = (bf16[1024,2048]{1,0:T(8,128)(2,1)}, bf16[1024,512]{1,0:T(8,128)(2,1)}, bf16[2,3,1024,128]{3,2,1,0:T(8,128)(2,1)}) custom-call(bf16[1024,2176]{1,0:T(8,128)(2,1)} %all-gather.8.cloned.1.call-done.x_ref, bf16[2048,768]{1,0:T(8,128)(2,1)} %bitcast.239, bf16[512,2048]{1,0:T(8,128)(2,1)} %bitcast.251, bf16[128,768]{1,0:T(8,128)(2,1)} %bitcast.287, ...), custom_call_target="tpu_custom_call" | custom-call | tf_op jit(solution)/shard_map/norm_qkv/pallas_call | solution.py:82
  218.2 6.0 %fusion.10 = (f32[2048,128]{1,0:T(8,128)}, f32[2048,128]{1,0:T(8,128)}) fusion(f32[128]{0:T(128)S(1)} %copy-done.32, f32[128]{0:T(128)S(1)} %copy-done.31, f32[2048]{0:T(1024)S(1)} %iota_convert_fusion), kind=kLoop, calls=%fused_computation.27 | loop fusion | flops 524288 | bytes 2106368 | tf_op jit(solution)/shard_map/mul | solution.py:351
  228.0 38.6 %attention.1 = bf16[4,2048,128]{2,1,0:T(8,128)(2,1)} custom-call(bf16[4,2048,128]{2,1,0:T(8,128)(2,1)} %bitcast.262, s32[8,2048]{1,0:T(8,128)} %broadcast_in_dim.70.idrow_ref, s32[2048,128]{1,0:T(8,128)} %broadcast_in_dim.71.idcol_ref, f32[2048,128]{1,0:T(8,128)} %get-tuple-element.109.cos_ref, f32[2048,128]{1,0:T(8,128)} %get-tuple-element.108.sin_ref), custom_call_target="tpu_custom_call" | custom-call | tf_op jit(solution)/shard_map/attention/pallas_call | solution.py:195
  268.9 2.1 collective-permute-done.3
  272.8 8.8 %copy.88 = bf16[4,2,2,288,1024]{4,3,2,0,1:T(8,128)(2,1)} copy(bf16[4,2,2,288,1024]{4,3,2,1,0:T(8,128)(2,1)} %bitcast.258) | data formatting | bytes 18874368 | tf_op jit(solution)/shard_map/reshape;reshape | solution.py:377
  281.6 6.6 %fusion.48 = (bf16[8,2,128,1024]{3,2,0,1:T(8,128)(2,1)}, bf16[8,2,128,1024]{3,2,0,1:T(8,128)(2,1)}) fusion(bf16[8,2,288,1024]{3,2,0,1:T(8,128)(2,1)} %bitcast.236), kind=kLoop, calls=%fused_computation.181 | loop fusion | bytes 16777216 | tf_op jit(solution)/shard_map/slice | solution.py:507
  291.2 6.5 %copy.90 = bf16[8,2,2,64,1024]{4,2,3,1,0:T(2,128)(2,1)S(1)} copy(bf16[8,2,2,64,1024]{4,3,2,0,1:T(8,128)(2,1)} %bitcast.254) | data formatting | bytes 8388608 | tf_op jit(solution)/shard_map/reshape | solution.py:507
  297.8 3.5 copy.112
  301.3 2.4 copy.89
  305.1 59.1 %feed_forward_both_ways.1 = (bf16[1024,2048]{1,0:T(8,128)(2,1)}, bf16[1024,2048]{1,0:T(8,128)(2,1)}, bf16[1024,128]{1,0:T(8,128)(2,1)}, f32[128,1024]{1,0:T(8,12...) custom-call(bf16[1024,2048]{1,0:T(8,128)(2,1)} %get-tuple-element.24.hb_ref, ...), custom_call_target="tpu_custom_call" | custom-call | tf_op jit(solution)/shard_map/feed_forward_both_ways/pallas_call | solution.py:280
  364.9 3.6 all-to-all-start
  370.3 4.6 all-to-all-done
  375.7 4.9 all-to-all-start.1
  382.5 9.9 %all-to-all-done.1 = bf16[8,128,128]{2,1,0:T(8,128)(2,1)S(1)} async-done(((bf16[8,128,128]{2,1,0:T(8,128)(2,1)}), bf16[8,128,128]{2,1,0:T(8,128)(2,1)S(1)}, u32[]{:S(2)}, u32[]{:S(2)}) %all-to-all-start.1) | async-done | bytes 262176 | tf_op jit(solution)/shard_map/all_to_all | solution.py:545
  393.1 3.3 adapter_grads.1
  407.4 18.9 %all_to_all.20 = bf16[8,40,1024]{2,1,0:T(8,128)(2,1)S(1)} all-to-all(bf16[8,40,1024]{2,1,0:T(8,128)(2,1)S(1)} %add_convert_fusion), channel_id=1, replica_groups=mesh['xl'=2,'z'=4,'c'=2,'y'=4,'xh'=2] {'y','xh'}, dimensions={0} | all-to-all | bytes 1310720 | tf_op jit(solution)/shard_map/all_to_all | solution.py:558
  427.6 4.9 all-to-all-start.3
  434.1 30.2 %all-to-all-done.3 = bf16[16,40,1024]{2,1,0:T(8,128)(2,1)S(1)} async-done(((bf16[16,40,1024]{2,1,0:T(8,128)(2,1)}), bf16[16,40,1024]{2,1,0:T(8,128)(2,1)S(1)}, u32[]{:S(2)}, u32[]{:S(2)}) %all-to-all-start.3) | async-done | bytes 1310752 | tf_op jit(solution)/shard_map/all_to_all | solution.py:560
  489.3 2.9 fusion.20
  (260 shorter events, 96.8 us)
Async XLA Ops:
  7.2 9.1 %copy-start.21 = (bf16[1,3,16,2048]{3,2,1,0:T(8,128)(2,1)S(1)}, bf16[1,3,16,2048]{3,2,1,0:T(8,128)(2,1)}, u32[]{:S(2)}) copy-start(bf16[1,3,16,2048]{3,2,1,0:T(8,128)(2,1)} %param.47) | copy-start | bytes 589828
  7.2 9.1 %copy-start.24 = (bf16[1,16,2048]{2,1,0:T(8,128)(2,1)S(1)}, bf16[1,16,2048]{2,1,0:T(8,128)(2,1)}, u32[]{:S(2)}) copy-start(bf16[1,16,2048]{2,1,0:T(8,128)(2,1)} %param.51) | copy-start | bytes 196612
  7.2 9.5 %copy-start.22 = (bf16[1,3,16,2048]{3,2,1,0:T(8,128)(2,1)S(1)}, bf16[1,3,16,2048]{3,2,1,0:T(8,128)(2,1)}, u32[]{:S(2)}) copy-start(bf16[1,3,16,2048]{3,2,1,0:T(8,128)(2,1)} %param.48) | copy-start | bytes 589828
  7.2 85.5 %all-gather.8.cloned.1.call-start = ((), (), s32[]{:S(2)}) async-start(), calls=%async_computation.6 | async-start | bytes 5013504 | tf_op jit(solution)/shard_map/all_gather | solution.py:486
  8.0 10.0 %copy-start.27 = (bf16[1,16,2048]{2,1,0:T(8,128)(2,1)S(1)}, bf16[1,16,2048]{2,1,0:T(8,128)(2,1)}, u32[]{:S(2)}) copy-start(bf16[1,16,2048]{2,1,0:T(8,128)(2,1)} %param.50) | copy-start | bytes 196612
  10.0 128.0 %all-gather.10.cloned.1.call-start = ((), (), s32[]{:S(2)}) async-start(), calls=%async_computation.9 | async-start | bytes 8257536 | tf_op jit(solution)/shard_map/all_gather | solution.py:375
  18.0 26.0 %collective-permute-start = (bf16[192,1024]{1,0:T(8,128)(2,1)S(1)}, bf16[192,1024]{1,0:T(8,128)(2,1)S(1)}, u32[]{:S(2)}, u32[]{:S(2)}) collective-permute-start(bf16[192,1024]{1,0:T(8,128)(2,1)S(1)} %constant_dynamic-update-slice_fusion.8), channel_id=1, source_target_pairs={{0,1},{1,0},{2,3},{3,2},{4,5},{5,4},{6,7},{7,6},{8,9},{9,8},{10,11... | collective-permute-start | bytes 1179656 | tf_op jit(solution)/shard_map/ppermute | solution.py:367
  22.7 21.2 %collective-permute-start.1 = (bf16[64,1024]{1,0:T(8,128)(2,1)S(1)}, bf16[64,1024]{1,0:T(8,128)(2,1)S(1)}, u32[]{:S(2)}, u32[]{:S(2)}) collective-permute-start(bf16[64,1024]{1,0:T(8,128)(2,1)S(1)} %pad_maximum_fusion.7), channel_id=1, source_target_pairs={{0,1},{1,0},{2,3},{3,2},{4,5},{5,4},{6,7},{7,6},{8,9},{9,8},{10,11... | collective-permute-start | bytes 393224 | tf_op jit(solution)/shard_map/ppermute | solution.py:472
  43.9 9.6 %copy-start.19 = (bf16[1,16,8192]{2,1,0:T(8,128)(2,1)S(1)}, bf16[1,16,8192]{2,1,0:T(8,128)(2,1)}, u32[]{:S(2)}) copy-start(bf16[1,16,8192]{2,1,0:T(8,128)(2,1)} %param.52) | copy-start | bytes 786436
  43.9 9.6 %copy-start.20 = (bf16[1,16,8192]{2,1,0:T(8,128)(2,1)S(1)}, bf16[1,16,8192]{2,1,0:T(8,128)(2,1)}, u32[]{:S(2)}) copy-start(bf16[1,16,8192]{2,1,0:T(8,128)(2,1)} %param.53) | copy-start | bytes 786436
  44.0 11.7 %copy-start.28 = (bf16[1,16,2048]{2,1,0:T(8,128)(2,1)S(1)}, bf16[1,16,2048]{2,1,0:T(8,128)(2,1)}, u32[]{:S(2)}) copy-start(bf16[1,16,2048]{2,1,0:T(8,128)(2,1)} %param.54) | copy-start | bytes 196612
  45.0 147.1 %all-gather.12.cloned.1.call-start = ((), (), s32[]{:S(2)}) async-start(), calls=%async_computation.10 | async-start | bytes 4718592 | tf_op jit(solution)/shard_map/all_gather | solution.py:488
  45.8 227.0 %all-gather.14.cloned.1.call-start = ((), (), s32[]{:S(2)}) async-start(), calls=%async_computation.11 | async-start | bytes 10616832 | tf_op jit(solution)/shard_map/all_gather | solution.py:375
  55.7 31.0 %copy-start.31 = (f32[128]{0:T(128)S(1)}, f32[128]{0:T(128)}, u32[]{:S(2)}) copy-start(f32[128]{0:T(128)} %constant.366.clone) | copy-start | bytes 1540
  55.8 29.5 %collective-permute-start.4 = (bf16[288,1024]{1,0:T(8,128)(2,1)S(1)}, bf16[288,1024]{1,0:T(8,128)(2,1)S(1)}, u32[]{:S(2)}, u32[]{:S(2)}) collective-permute-start(bf16[288,1024]{1,0:T(8,128)(2,1)S(1)} %constant_dynamic-update-slice_fusion.13), channel_id=1, source_target_pairs={{0,1},{1,0},{2,3},{3,2},{4,5},{5,4},{6,7},{7,6},{8,9},{9,8},{10,11... | collective-permute-start | bytes 1769480 | tf_op jit(solution)/shard_map/ppermute | solution.py:367
  86.5 401.3 %reduce-scatter.5.cloned.1.call-start = ((), (), s32[]{:S(2)}) async-start(), calls=%async_computation.8 | async-start | bytes 4718592 | tf_op jit(solution)/shard_map/reduce_scatter | solution.py:541
  201.4 14.5 %copy-start.8 = (bf16[2,1024,128]{2,1,0:T(8,128)(2,1)S(1)}, bf16[2,1024,128]{2,1,0:T(8,128)(2,1)}, u32[]{:S(2)}) copy-start(bf16[2,1024,128]{2,1,0:T(8,128)(2,1)} %get-tuple-element.28) | copy-start | bytes 1572868
  216.0 8.2 %copy-start.3 = (bf16[2,3,1024,128]{3,2,1,0:T(8,128)(2,1)S(1)}, bf16[2,3,1024,128]{3,2,1,0:T(8,128)(2,1)}, u32[]{:S(2)}) copy-start(bf16[2,3,1024,128]{3,2,1,0:T(8,128)(2,1)} %get-tuple-element.27) | copy-start | bytes 4718596
  217.3 6.8 %collective-permute-start.2 = (bf16[4,1024,128]{2,1,0:T(8,128)(2,1)S(1)}, bf16[4,1024,128]{2,1,0:T(8,128)(2,1)S(1)}, u32[]{:S(2)}, u32[]{:S(2)}) collective-permute-start(bf16[4,1024,128]{2,1,0:T(8,128)(2,1)S(1)} %fusion.15), channel_id=1, source_target_pairs={{0,8},{8,0},{1,9},{9,1},{2,10},{10,2},{3,11},{11,3},{4,12},{12,4},... | collective-permute-start | bytes 3145736 | tf_op jit(solution)/shard_map/ppermute | solution.py:522
  268.2 2.7 collective-permute-start.3
  364.2 125.0 %reduce-scatter.3.cloned.1.call-start = ((), (), s32[]{:S(2)}) async-start(), calls=%async_computation.7 | async-start | bytes 4718592 | tf_op jit(solution)/shard_map/reduce_scatter | solution.py:540
  364.8 17.6 %copy-start.18 = (f32[128,768]{1,0:T(8,128)S(1)}, f32[128,768]{1,0:T(8,128)}, u32[]{:S(2)}) copy-start(f32[128,768]{1,0:T(8,128)} %get-tuple-element.33) | copy-start | bytes 1179652
  364.8 17.6 %copy-start.23 = (f32[128,256]{1,0:T(8,128)S(1)}, f32[128,256]{1,0:T(8,128)}, u32[]{:S(2)}) copy-start(f32[128,256]{1,0:T(8,128)} %get-tuple-element.34) | copy-start | bytes 393220
  364.9 10.1 %all-to-all-start = ((bf16[8,128,128]{2,1,0:T(8,128)(2,1)}), bf16[8,128,128]{2,1,0:T(8,128)(2,1)S(1)}, u32[]{:S(2)}, u32[]{:S(2)}) async-start(bf16[8,128,128]{2,1,0:T(8,128)(2,1)} %bitcast.74), calls=%async_computation.2 | async-start | bytes 524288 | tf_op jit(solution)/shard_map/all_to_all | solution.py:543
  375.7 16.7 %all-to-all-start.1 = ((bf16[8,128,128]{2,1,0:T(8,128)(2,1)}), bf16[8,128,128]{2,1,0:T(8,128)(2,1)S(1)}, u32[]{:S(2)}, u32[]{:S(2)}) async-start(bf16[8,128,128]{2,1,0:T(8,128)(2,1)} %broadcast_in_dim.74), calls=%async_computation.3 | async-start | bytes 524288 | tf_op jit(solution)/shard_map/all_to_all | solution.py:545
  403.7 2.4 collective-permute-start.5
  426.3 6.2 %copy-start.2 = (bf16[1,128,2048]{2,1,0:T(8,128)(2,1)S(1)}, bf16[1,128,2048]{2,1,0:T(8,128)(2,1)}, u32[]{:S(2)}) copy-start(bf16[1,128,2048]{2,1,0:T(8,128)(2,1)} %param.29) | copy-start | bytes 1572868
  427.6 36.6 %all-to-all-start.3 = ((bf16[16,40,1024]{2,1,0:T(8,128)(2,1)}), bf16[16,40,1024]{2,1,0:T(8,128)(2,1)S(1)}, u32[]{:S(2)}, u32[]{:S(2)}) async-start(bf16[16,40,1024]{2,1,0:T(8,128)(2,1)} %broadcast_in_dim.75), calls=%async_computation.5 | async-start | bytes 2621440 | tf_op jit(solution)/shard_map/all_to_all | solution.py:560
  432.6 31.6 %copy-start.29 = (f32[128]{0:T(128)}, f32[128]{0:T(128)S(1)}, u32[]{:S(2)}) copy-start(f32[128]{0:T(128)S(1)} %broadcast_multiply_fusion.2) | copy-start | bytes 1540
  482.5 5.3 %copy-start.30 = (f32[128]{0:T(128)S(1)}, f32[128]{0:T(128)}, u32[]{:S(2)}) copy-start(f32[128]{0:T(128)} %copy-done.29) | copy-start | bytes 1540
  482.8 6.4 %copy-start.6 = (bf16[1,128,2048]{2,1,0:T(8,128)(2,1)S(1)}, bf16[1,128,2048]{2,1,0:T(8,128)(2,1)}, u32[]{:S(2)}) copy-start(bf16[1,128,2048]{2,1,0:T(8,128)(2,1)} %param.30) | copy-start | bytes 1572868
  482.9 6.4 %copy-start.26 = (f32[1,2,8,128]{3,1,2,0:T(2,128)S(1)}, f32[1,2,8,128]{3,1,2,0:T(2,128)}, u32[]{:S(2)}) copy-start(f32[1,2,8,128]{3,1,2,0:T(2,128)} %copy.115) | copy-start | bytes 24580
  (17 other events, 47.5 us)
Sparse Core Ops, SparseCore 0:
  10.1 82.5 all-gather.7
  94.4 43.5 all-gather.9
  139.6 52.4 all-gather.11
  193.7 53.1 all-gather.13
  364.4 58.5 reduce-scatter.4
  425.2 63.9 reduce-scatter.2
